TPU v7x, 512 devices: a whole 4x4x16 slice. The times are simulated.
512 devices in a mesh: dp: 4 (over x), fsdp: 32 (over z, core), tensor: 4 (over y).
Axes of the slice: x: 4, y: 4, z: 16, core: 2. Of those that a mesh axis runs over, the one named last changes fastest.
Arguments:
- momentum: float32 [4096, 8192], P('fsdp', 'tensor'), may hold values from -60 to 60
- grads: bfloat16 [4, 4096, 8192], P('dp', 'fsdp', 'tensor'), may hold values from -40 to 40
- right_basis: bfloat16 [8192, 512], P('tensor', 'fsdp'), may hold values from -0.0625 to 0.0625
Outputs:
- new_momentum: float32 [4096, 8192], P('fsdp', 'tensor')
- update: bfloat16 [4096, 8192], P('fsdp', 'tensor')
- new_basis: bfloat16 [8192, 512], P('tensor', 'fsdp')
All inputs are finite; a program needn't handle non-finite values.
Results may differ from a plain program's by a relative error of at most 0.0016.
Values may be sent and summed in bfloat16 or wider, within the bound.
No kernel may reach another device: no remote copies, remote signals or barrier semaphores. Data moves between devices by JAX's collectives and lax.ppermute only.
A program may use at most 64 MiB of HBM per device.

v0:
```python
import math

import jax
import jax.numpy as jnp
from jax import lax
from jax.sharding import PartitionSpec as P

HIGH = lax.Precision.HIGHEST


def column_scale(squares):
    summed = lax.psum(squares, "tensor")
    return lax.rsqrt(summed + 1e-06)


def left_total(partial_left):
    return lax.psum(partial_left, "tensor")


def per_device(momentum, grads, right_basis):
    local_cols = momentum.shape[1]
    summed = lax.psum(grads[0].astype(jnp.float32), "dp")
    total = momentum + summed
    rank_local = right_basis.shape[1]
    fsdp_count = lax.axis_size("fsdp")
    rank_all = rank_local * fsdp_count
    factor_scale = math.sqrt(
        momentum.shape[0] * fsdp_count * local_cols * lax.axis_size("tensor") / rank_all
    )
    rows_used = lax.all_gather(right_basis, "fsdp", axis=1, tiled=True)
    partial_left = jnp.dot(total, rows_used.astype(jnp.float32), precision=HIGH)
    left = left_total(partial_left)
    gram = lax.psum(jnp.dot(left.T, left, precision=HIGH), "fsdp")
    factor = jnp.linalg.cholesky(gram)
    left_basis = jax.scipy.linalg.solve_triangular(factor, left.T, lower=True).T
    offset = lax.axis_index("fsdp") * rank_local
    right_part = lax.psum_scatter(
        lax.dot_general(left_basis, total, (((0,), (0,)), ((), ())), precision=HIGH),
        "fsdp",
        scatter_dimension=0,
        tiled=True,
    )
    right_t = lax.all_gather(right_part, "fsdp", axis=0, tiled=True)
    norms = column_scale(jnp.sum(right_t * right_t, axis=1))
    scaled_t = right_t * norms[:, None]
    new_momentum = total - 0.05 * jnp.dot(left_basis, right_t, precision=HIGH)
    update = (factor_scale * jnp.dot(left_basis, scaled_t, precision=HIGH)).astype(jnp.bfloat16)
    new_basis = lax.dynamic_slice_in_dim(scaled_t, offset, rank_local, 0).T.astype(jnp.bfloat16)
    return (new_momentum, update, new_basis)


def solution(mesh):
    in_specs = (P("fsdp", "tensor"), P("dp", "fsdp", "tensor"), P("tensor", "fsdp"))
    out_specs = (P("fsdp", "tensor"), P("fsdp", "tensor"), P("tensor", "fsdp"))
    return jax.shard_map(
        per_device, mesh=mesh, in_specs=in_specs, out_specs=out_specs, check_vma=False
    )
```

profile of v0, /device:TPU:2, one launch (start us, length us, event | category | flops | bytes accessed | tf_op | source)
XLA Modules:
  0.0 732.8 jit_solution(1090216649150598057)
XLA Ops:
  8.0 2.1 bitcast_convert_fusion
  10.2 0.5 all-gather.3.cloned.1.call-update
  10.8 65.9 %all-reduce.5.cloned.1.call-done = f32[128,2048]{1,0:T(8,128)} async-done(((f32[128,2048]{1,0:T(8,128)}), f32[128,2048]{1,0:T(8,128)}) %all-reduce.5.cloned.1.call-update) | async-done | bytes 1048592 | tf_op jit(solution)/shard_map/psum | solution.py:22
  76.7 1.7 add.63
  78.4 11.1 %all-gather.3.cloned.1.call-done = bf16[2048,512]{0,1:T(8,128)(2,1)} async-done(((bf16[2048,16]{0,1:T(8,128)(2,1)}), bf16[2048,512]{0,1:T(8,128)(2,1)}) %all-gather.3.cloned.1.call-update) | async-done | bytes 2097168 | tf_op jit(solution)/shard_map/all_gather | solution.py:30
  89.5 4.5 fusion.38
  94.0 54.3 %all-reduce.7.cloned.1.call-done = f32[128,512]{1,0:T(8,128)} async-done(((f32[128,512]{1,0:T(8,128)}), f32[128,512]{1,0:T(8,128)}) %all-reduce.7.cloned.1.call-update) | async-done | bytes 262160 | tf_op jit(solution)/shard_map/psum | solution.py:17
  148.4 3.0 fusion.39
  151.7 210.2 %all-reduce.9.cloned.1.call-done = f32[512,512]{0,1:T(8,128)} async-done(((f32[512,512]{0,1:T(8,128)}), f32[512,512]{0,1:T(8,128)}) %all-reduce.9.cloned.1.call-update) | async-done | bytes 1048592 | tf_op jit(solution)/shard_map/psum | solution.py:33
  361.8 1.6 copy.7
  363.4 1.4 fusion.2
  364.9 11.7 %cholesky.104 = f32[128,128]{1,0:T(8,128)S(1)} custom-call(f32[128,128]{1,0:T(8,128)S(1)} %cholesky.266), custom_call_target="Cholesky" | custom-call | tf_op jit(solution)/shard_map/jit(cholesky)/cholesky | solution.py:34
  376.7 9.8 %custom-call.31 = f32[1,128,128]{1,2,0:T(8,128)S(1)} custom-call(f32[1,128,128]{2,1,0:T(8,128)S(1)} %get-tuple-element.30), custom_call_target="InvertDiagBlocksLowerTriangular" | custom-call | tf_op jit(solution)/shard_map/jit(cholesky)/cholesky | solution.py:34
  387.2 0.7 copy-done.2
  387.9 11.7 %cholesky.217 = f32[128,128]{1,0:T(8,128)S(1)} custom-call(f32[128,128]{1,0:T(8,128)S(1)} %cholesky.270), custom_call_target="Cholesky" | custom-call | tf_op jit(solution)/shard_map/jit(cholesky)/cholesky | solution.py:34
  399.6 10.0 %custom-call.32 = f32[1,128,128]{1,2,0:T(8,128)S(1)} custom-call(f32[1,128,128]{2,1,0:T(8,128)S(1)} %get-tuple-element.27), custom_call_target="InvertDiagBlocksLowerTriangular" | custom-call | tf_op jit(solution)/shard_map/jit(cholesky)/cholesky | solution.py:34
  409.7 1.2 convolution_dynamic-update-slice_fusion
  411.2 0.6 cholesky.275
  411.8 13.2 %cholesky.238 = f32[128,128]{1,0:T(8,128)} custom-call(f32[128,128]{1,0:T(8,128)} %cholesky.275), custom_call_target="Cholesky" | custom-call | tf_op jit(solution)/shard_map/jit(cholesky)/cholesky | solution.py:34
  425.0 1.5 select_reduce_fusion.1
  426.5 11.3 %custom-call.33 = f32[1,128,128]{1,2,0:T(8,128)} custom-call(f32[1,128,128]{2,1,0:T(8,128)} %get-tuple-element.24), custom_call_target="InvertDiagBlocksLowerTriangular" | custom-call | tf_op jit(solution)/shard_map/jit(cholesky)/cholesky | solution.py:34
  437.8 1.0 convolution_dynamic-update-slice_fusion.1
  438.8 0.4 convolution_subtract_fusion.5
  439.2 11.7 %cholesky.255 = f32[128,128]{1,0:T(8,128)S(1)} custom-call(f32[128,128]{1,0:T(8,128)S(1)} %convolution_subtract_fusion.5), custom_call_target="Cholesky" | custom-call | tf_op jit(solution)/shard_map/jit(cholesky)/cholesky | solution.py:34
  451.0 0.7 compare_reduce_fusion.1
  451.7 0.6 compare_reduce_fusion
  452.3 0.6 compare_reduce_fusion.2
  455.9 10.5 %while.1 = (s32[]{:T(128)}, f32[512,512]{1,0:T(8,128)S(1)}, s32[4,2]{0,1:T(2,128)S(1)}, f32[4,128,128]{2,1,0:T(8,128)}, s32[]{:T(128)}) while((s32[]{:T(128)}, f32[512,512]{1,0:T(8,128)S(1)}, s32[4,2]{0,1:T(2,128)S(1)}, f32[4,128,128]{2,1,0:T(8,128)}, s32[]{:T(128)}) %tuple.31), condition=%wide.while_cond, body=%wide.while_body.sunk | while | flops 2 | bytes 132205 | solution.py:35
  456.0 0.5 fusion.53
  456.5 2.0 bitcast_dynamic-update-slice_fusion.2
  458.6 0.5 fusion.53
  459.1 2.0 bitcast_dynamic-update-slice_fusion.2
  461.2 0.5 fusion.53
  461.7 2.0 bitcast_dynamic-update-slice_fusion.2
  463.8 0.5 fusion.53
  464.3 2.0 bitcast_dynamic-update-slice_fusion.2
  466.4 40.1 %custom-call.34 = f32[4,128,128]{1,2,0:T(8,128)S(1)} custom-call(f32[4,128,128]{2,1,0:T(8,128)} %get-tuple-element.10), custom_call_target="InvertDiagBlocksLowerTriangular" | custom-call | tf_op jit(solution)/shard_map/jit(_solve_triangular)/triangular_solve | solution.py:35
  507.4 0.4 convolution_subtract_fusion.2
  508.1 0.5 convolution_subtract_fusion.4
  508.8 5.0 fusion.31
  513.9 113.9 %reduce-scatter.2.cloned.1.call-done = f32[16,2048]{1,0:T(8,128)} async-done(((f32[512,2048]{1,0:T(8,128)}), f32[16,2048]{1,0:T(8,128)}) %reduce-scatter.2.cloned.1.call-update) | async-done | bytes 131088 | tf_op jit(solution)/shard_map/reduce_scatter | solution.py:37
  627.8 74.3 %all-gather.5.cloned.1.call-done = f32[512,2048]{1,0:T(8,128)} async-done(((f32[16,2048]{1,0:T(8,128)}), f32[512,2048]{1,0:T(8,128)}) %all-gather.5.cloned.1.call-update) | async-done | bytes 4194320 | tf_op jit(solution)/shard_map/all_gather | solution.py:43
  702.0 2.5 multiply_reduce_fusion
  704.6 10.5 %psum.31 = f32[512]{0:T(512)S(1)} all-reduce(f32[512]{0:T(512)S(1)} %multiply_reduce_fusion), channel_id=1, replica_groups=mesh['dp'=4,'fsdp'=32,'tensor'=4] {'tensor'}, use_global_device_ids=true, to_apply=%region_13.14 | all-reduce | flops 512 | bytes 4096 | tf_op jit(solution)/shard_map/psum | solution.py:12
  715.1 2.5 broadcast_multiply_fusion
  717.6 3.1 fusion.1
  720.7 0.6 fusion.19
  721.4 3.3 fusion
  (39 shorter events, 3.9 us)
Async XLA Ops:
  8.0 68.7 %all-reduce.5.cloned.1.call-start = ((), (), s32[]{:S(2)}) async-start(), calls=%async_computation.1 | async-start | bytes 2097152 | tf_op jit(solution)/shard_map/psum | solution.py:22
  10.2 79.3 %all-gather.3.cloned.1.call-start = ((), (), s32[]{:S(2)}) async-start(), calls=%async_computation.2 | async-start | bytes 2162688 | tf_op jit(solution)/shard_map/all_gather | solution.py:30
  10.8 137.6 %all-reduce.7.cloned.1.call-start = ((), (), s32[]{:S(2)}) async-start(), calls=%async_computation.3 | async-start | bytes 524288 | tf_op jit(solution)/shard_map/psum | solution.py:17
  94.0 267.8 %all-reduce.9.cloned.1.call-start = ((), (), s32[]{:S(2)}) async-start(), calls=%async_computation.4 | async-start | bytes 2097152 | tf_op jit(solution)/shard_map/psum | solution.py:33
  151.4 476.3 %reduce-scatter.2.cloned.1.call-start = ((), (), s32[]{:S(2)}) async-start(), calls=%async_computation.5 | async-start | bytes 4325376 | tf_op jit(solution)/shard_map/reduce_scatter | solution.py:37
  364.8 141.7 %copy-start.1 = (f32[128,512]{1,0:T(8,128)S(1)}, f32[128,512]{1,0:T(8,128)}, u32[]{:S(2)}) copy-start(f32[128,512]{1,0:T(8,128)} %all-reduce.7.cloned.1.call-done) | copy-start | bytes 786436
  387.2 0.7 copy-start.2
  513.8 188.2 %all-gather.5.cloned.1.call-start = ((), (), s32[]{:S(2)}) async-start(), calls=%async_computation.6 | async-start | bytes 4325376 | tf_op jit(solution)/shard_map/all_gather | solution.py:43
  717.6 3.8 copy-start
Sparse Core Ops, SparseCore 0:
  11.8 64.8 all-reduce.4
  94.1 54.2 all-reduce.6
Sparse Core Ops, SparseCore 1:
  13.0 76.4 all-gather.2
  151.5 210.3 all-reduce.8
  513.9 113.8 reduce-scatter.1
  630.1 71.9 all-gather.4
where the time goes:
time: 736 us; the launch traced here: 733 us
  waiting for transfers between devices  530 us (72%)
  other arithmetic  134 us (18%)
  matrix products  24.8 us (3%)
  between operations  18.9 us (3%)
  local copies, waits for them, and re-layouts  14.1 us (2%)
  blocking collectives  10.5 us (1%)
    psum x1, waiting for transfers between devices, per_device(): gram = lax.psum(jnp.dot(left.T, left, precision=HIGH), 'fsdp')  210 us
    reduce_scatter x1, waiting for transfers between devices, per_device(): lax.psum_scatter(lax.dot_general(left_basis, total, (((0,), (0,)), ((), (...  114 us
    another operation x14, other arithmetic, per_device(): factor = jnp.linalg.cholesky(gram)  83 us
    all_gather x1, waiting for transfers between devices, per_device(): right_t = lax.all_gather(right_part, 'fsdp', axis=0, tiled=True)  74.3 us
    psum x1, waiting for transfers between devices, per_device(): summed = lax.psum(grads[0].astype(jnp.float32), 'dp')  65.9 us
    psum x1, waiting for transfers between devices, left_total(): return lax.psum(partial_left, 'tensor')  54.3 us
    another operation x3, other arithmetic, per_device(): left_basis = jax.scipy.linalg.solve_triangular(factor, left.T, lower=True).T  40.5 us
  transfers between devices with their start and end apart: 6, of which 6 were waited for; matrix products, arithmetic and copies ran while one was open for 0% of the time, Pallas kernels for 0%

commit v1 on v0

v1 whole, which is shorter than its diff:
```python
import math

import jax
import jax.numpy as jnp
from jax import lax
from jax.experimental import pallas as pl
from jax.experimental.pallas import tpu as pltpu
from jax.sharding import PartitionSpec as P

HIGH = lax.Precision.HIGHEST
BOTH = ("dp", "tensor")
EDGE = 128


def invert_block(block):
    size = block.shape[0]
    steps = size // 8
    sub = lax.broadcasted_iota(jnp.int32, (8, size), 0)
    lane = lax.broadcasted_iota(jnp.int32, (8, size), 1)
    full = (8, size)
    rows = [block[8 * i : 8 * i + 8] for i in range(steps)]
    done = []
    for k in range(steps):
        here = (lane >= 8 * k) & (lane < 8 * k + 8)
        columns = [[jnp.broadcast_to(r[:, 8 * k + m : 8 * k + m + 1], full) for m in range(8)] for r in rows[k:]]
        cur = jnp.where(here, (lane - 8 * k == sub).astype(jnp.float32), rows[k])
        col = columns[0]
        result = jnp.zeros(full, jnp.float32)
        for j in range(8):
            at = sub == j
            pivot = jnp.broadcast_to(col[j][j : j + 1], full)
            row = jnp.broadcast_to(cur[j : j + 1], full)
            result = jnp.where(at, row * lax.rsqrt(pivot), result)
            recip = 1.0 / pivot
            mult = jnp.where(at, -1.0, col[j])
            cur = jnp.where(at, 0.0, cur) - (mult * row) * recip
            for m in range(j + 1, 8):
                lead = jnp.broadcast_to(col[m][j : j + 1], full)
                col[m] = jnp.where(at, 0.0, col[m]) - (mult * lead) * recip
        done.append(jnp.where(lane <= 8 * k + sub, result, 0.0))
        if k + 1 < steps:
            spread = [jnp.broadcast_to(cur[m : m + 1], full) for m in range(8)]
            for i in range(k + 1, steps):
                acc = jnp.where(here, 0.0, rows[i])
                for m in range(8):
                    acc = acc - columns[i - k][m] * spread[m]
                rows[i] = acc
    return jnp.concatenate(done, axis=0)


def invert_kernel(gram_ref, out_ref, work):
    size = gram_ref.shape[0]
    count = size // EDGE
    work[...] = gram_ref[...]
    out_ref[...] = jnp.zeros_like(out_ref)
    for k in range(count):
        a, b = k * EDGE, (k + 1) * EDGE
        inv = invert_block(work[a:b, a:b])
        if k:
            out_ref[a:b, :a] = jnp.dot(inv, work[a:b, :a], precision=HIGH, preferred_element_type=jnp.float32)
        out_ref[a:b, a:b] = inv
        if b < size:
            upper = jnp.dot(inv, work[a:b, b:], precision=HIGH, preferred_element_type=jnp.float32)
            full = jnp.concatenate([out_ref[a:b, :b], upper], axis=1)
            work[b:, a:b] = jnp.zeros((size - b, EDGE), jnp.float32)
            work[b:, :] -= lax.dot_general(upper, full, (((0,), (0,)), ((), ())), precision=HIGH, preferred_element_type=jnp.float32)


def inverse_factor(gram):
    rank = gram.shape[0]
    return pl.pallas_call(
        invert_kernel,
        out_shape=jax.ShapeDtypeStruct((rank, rank), jnp.float32),
        in_specs=[pl.BlockSpec(memory_space=pltpu.VMEM)],
        out_specs=pl.BlockSpec(memory_space=pltpu.VMEM),
        scratch_shapes=[pltpu.VMEM((rank, rank), jnp.float32)],
        compiler_params=pltpu.CompilerParams(vmem_limit_bytes=16 * 1024 * 1024),
        cost_estimate=pl.CostEstimate(flops=20 * 10**9, bytes_accessed=2 * 4 * rank * rank, transcendentals=0),
        name="inverse_factor",
    )(gram)


def dot(a, b, dims):
    return lax.dot_general(a, b, (dims, ((), ())), precision=HIGH, preferred_element_type=jnp.float32)


def swap(x, axis, groups=None):
    return lax.all_to_all(x, axis, 0, 0, tiled=True, axis_index_groups=groups)


def share(x, n, axis, groups=None):
    return swap(jnp.broadcast_to(x[None], (n,) + x.shape), axis, groups)


def per_device(momentum, grads, right_basis):
    rows, local_cols = momentum.shape
    n_dp, n_fsdp, n_tensor = (lax.axis_size(a) for a in ("dp", "fsdp", "tensor"))
    n_both = n_dp * n_tensor
    n_z = n_fsdp // 2
    near = 4
    far = n_z // near
    rank_local = right_basis.shape[1]
    rank = rank_local * n_fsdp
    cols = local_cols // n_dp
    half = cols // 2
    factor_scale = math.sqrt(rows * n_fsdp * local_cols * n_tensor / rank)
    cores = [[2 * z, 2 * z + 1] for z in range(n_z)]
    zs = [[2 * z + c for z in range(n_z)] for c in range(2)]
    nears = [[2 * (near * h + l) + c for l in range(near)] for h in range(far) for c in range(2)]
    fars = [[2 * (near * h + l) + c for h in range(far)] for l in range(near) for c in range(2)]
    d = lax.axis_index("dp")
    slot = d * n_tensor + lax.axis_index("tensor")
    me = lax.axis_index("fsdp")

    with jax.named_scope("basis"):
        mine = lax.dynamic_slice_in_dim(right_basis.T, d * cols, cols, 1)
        pair = swap(mine.reshape(rank_local, 2, half).transpose(1, 0, 2), "fsdp", cores)
        part = share(pair.reshape(2 * rank_local, half), n_z, "fsdp", zs)
        basis_t = share(part.reshape(rank, half), 2, "fsdp", cores).transpose(1, 0, 2).reshape(rank, cols)
    with jax.named_scope("total"):
        blocks = swap(grads[0].reshape(rows, n_dp, cols).transpose(1, 0, 2), "dp")
        total = lax.dynamic_slice_in_dim(momentum, d * cols, cols, 1) + jnp.sum(blocks.astype(jnp.float32), axis=0)
    with jax.named_scope("left"):
        partial = dot(total, basis_t.astype(jnp.float32), ((1,), (1,)))
        partial = jnp.sum(swap(partial.reshape(n_dp, rows // n_dp, rank), "dp"), axis=0)
        partial = jnp.sum(share(partial, n_tensor, "tensor"), axis=0)
        left = share(partial, n_dp, "dp").reshape(rows, rank)
    with jax.named_scope("product"):
        prod = dot(left, total, ((0,), (0,)))
        prod = jnp.sum(swap(prod.reshape(rank, 2, half).transpose(1, 0, 2), "fsdp", cores), axis=0)
        prod = lax.psum_scatter(prod, "fsdp", scatter_dimension=0, tiled=True, axis_index_groups=zs)
    with jax.named_scope("gram"):
        gram = dot(left, left, ((0,), (0,)))
        gram = lax.dynamic_slice_in_dim(gram, slot * (rank // n_both), rank // n_both, 0)
        gram = jnp.sum(swap(gram.reshape(2, rank // n_both // 2, rank), "fsdp", cores), axis=0)
        gram = jnp.sum(share(gram, near, "fsdp", nears), axis=0)
        gram = jnp.sum(share(gram, far, "fsdp", fars), axis=0)
        gram = share(gram, 2, "fsdp", cores).reshape(rank // n_both, rank)
        gram = share(gram, n_both, BOTH).reshape(rank, rank)
    with jax.named_scope("factor"):
        inverse = inverse_factor(gram)
        prod, inverse = lax.optimization_barrier((prod, inverse))
    with jax.named_scope("right"):
        prod = lax.all_gather(prod, "fsdp", axis=0, tiled=True, axis_index_groups=zs)
        prod = share(prod, 2, "fsdp", cores).transpose(1, 0, 2).reshape(rank, cols)
        left_basis = dot(left, inverse, ((1,), (1,)))
        right_t = dot(inverse, prod, ((1,), (0,)))
    with jax.named_scope("norms"):
        squares = jnp.sum(right_t * right_t, axis=1)
        norms = lax.rsqrt(jnp.sum(share(squares, n_both, BOTH), axis=0) + 1e-06)
        scaled_t = right_t * norms[:, None]
    with jax.named_scope("outputs"):
        new_momentum = total - 0.05 * dot(left_basis, right_t, ((1,), (0,)))
        update = (factor_scale * dot(left_basis, scaled_t, ((1,), (0,)))).astype(jnp.bfloat16)
        basis = lax.dynamic_slice_in_dim(scaled_t, me * rank_local, rank_local, 0).astype(jnp.bfloat16)
        new_momentum = share(new_momentum, n_dp, "dp").transpose(1, 0, 2).reshape(rows, local_cols)
        pack = share(jnp.concatenate([update, basis], axis=0), n_dp, "dp").transpose(1, 0, 2).reshape(rows + rank_local, local_cols)
    return (new_momentum, pack[:rows], pack[rows:].T)


def solution(mesh):
    in_specs = (P("fsdp", "tensor"), P("dp", "fsdp", "tensor"), P("tensor", "fsdp"))
    out_specs = (P("fsdp", "tensor"), P("fsdp", "tensor"), P("tensor", "fsdp"))
    return jax.shard_map(
        per_device, mesh=mesh, in_specs=in_specs, out_specs=out_specs, check_vma=False
    )
```

time: 736 us -> 312 us (0.42)
  waiting for transfers between devices: 530 us -> 111 us
  other arithmetic: 134 us -> 2.23 us
  blocking collectives: 10.5 us -> 84.5 us
  starting transfers between devices: 0.43 us -> 53.7 us
  Pallas kernels: 0 us -> 20.5 us
  matrix products: 24.8 us -> 8.22 us
    psum x3 -> x0, waiting for transfers between devices: 330 us -> none  [the longest x1 210 us: per_device(): gram = lax.psum(jnp.dot(left.T, left, precision=HIGH), 'fsdp')]
    another operation x17 -> x0, other arithmetic: 123 us -> none  [the longest x14 83 us: per_device(): factor = jnp.linalg.cholesky(gram)]
    reduce_scatter x1 -> x0, waiting for transfers between devices: 114 us -> none  [per_device(): lax.psum_scatter(lax.dot_general(left_basis, total, (((0,), (0,)), ((), (...]
    all_gather x2 -> x0, waiting for transfers between devices: 85.4 us -> none  [the longest x1 74.3 us: per_device(): right_t = lax.all_gather(right_part, 'fsdp', axis=0, tiled=True)]
    all_to_all x0 -> x10, waiting for transfers between devices: none -> 64.4 us  [swap(): return lax.all_to_all(x, axis, 0, 0, tiled=True, axis_index_groups=groups)]
    all_to_all x0 -> x7, blocking collectives: none -> 54.1 us  [swap(): return lax.all_to_all(x, axis, 0, 0, tiled=True, axis_index_groups=groups)]
    all_to_all x0 -> x10, starting transfers between devices: none -> 53.7 us  [swap(): return lax.all_to_all(x, axis, 0, 0, tiled=True, axis_index_groups=groups)]
    unnamed x6 -> x2, waiting for transfers between devices: 0.6 us -> 46.6 us
  transfers between devices with their start and end apart: 6 -> 11, of which waited for: 6 -> 9; matrix products, arithmetic and copies ran while one was open for 0% -> 4% of each run, Pallas kernels for 0% -> 0%
where the time goes in v1:
time: 312 us; the launch traced here: 310 us
  waiting for transfers between devices  111 us (36%)
  blocking collectives  84.5 us (27%)
  starting transfers between devices  53.7 us (17%)
  Pallas kernels  20.5 us (7%)
  local copies, waits for them, and re-layouts  15.9 us (5%)
  between operations  14.3 us (5%)
  matrix products  8.22 us (3%)
    all_to_all x10, waiting for transfers between devices, swap(): return lax.all_to_all(x, axis, 0, 0, tiled=True, axis_index_groups=groups)  64.4 us
    all_to_all x7, blocking collectives, swap(): return lax.all_to_all(x, axis, 0, 0, tiled=True, axis_index_groups=groups)  54.1 us
    all_to_all x10, starting transfers between devices, swap(): return lax.all_to_all(x, axis, 0, 0, tiled=True, axis_index_groups=groups)  53.7 us
    unnamed x2, waiting for transfers between devices  46.6 us
    all_gather x1, blocking collectives, per_device(): lax.all_gather(prod, 'fsdp', axis=0, tiled=True, axis_index_groups=zs)  30.3 us
    pallas_call x1, Pallas kernels, inverse_factor(): pl.pallas_call(invert_kernel, out_shape=jax.ShapeDtypeStruct((rank, rank)...  20.5 us
    dot_general x7, matrix products, dot(): lax.dot_general(a, b, (dims, ((), ())), precision=HIGH, preferred_element...  8.22 us
    broadcast_in_dim x12, local copies, waits for them, and re-layouts, share(): return swap(jnp.broadcast_to(x[None], (n,) + x.shape), axis, groups)  6.67 us
  transfers between devices with their start and end apart: 11, of which 9 were waited for; matrix products, arithmetic and copies ran while one was open for 4% of the time, Pallas kernels for 0%

profile of v1, /device:TPU:2, one launch (start us, length us, event | category | flops | bytes accessed | tf_op | source)
XLA Modules:
  0.0 310.4 jit_solution(15836062067440948940)
XLA Ops:
  7.2 0.8 copy-done
  8.6 3.2 %all-to-all-start.1 = ((bf16[2,16,256]{2,1,0:T(8,128)(2,1)}), bf16[2,16,256]{2,1,0:T(8,128)(2,1)S(1)}, u32[]{:S(2)}, u32[]{:S(2)}) async-start(bf16[2,16,256]{2,1,0:T(8,128)(2,1)} %copy.50), calls=%async_computation.1 | async-start | bytes 32768 | tf_op jit(solution)/shard_map/basis/all_to_all | solution.py:88
  11.9 1.3 copy.48
  13.4 17.3 %all_to_all.86 = bf16[4,128,512]{2,1,0:T(8,128)(2,1)S(1)} all-to-all(bf16[4,128,512]{2,1,0:T(8,128)(2,1)S(1)} %copy.49), channel_id=1, replica_groups=mesh['dp'=4,'fsdp'=32,'tensor'=4] {'dp'}, dimensions={0} | all-to-all | bytes 1048576 | tf_op jit(solution)/shard_map/total/all_to_all | solution.py:88
  30.7 0.7 broadcast_in_dim.31
  31.4 11.2 %all-to-all-start.2 = ((bf16[16,32,256]{2,1,0:T(8,128)(2,1)}), bf16[16,32,256]{2,1,0:T(8,128)(2,1)S(1)}, u32[]{:S(2)}, u32[]{:S(2)}) async-start(bf16[16,32,256]{2,1,0:T(8,128)(2,1)} %broadcast_in_dim.31), calls=%async_computation.2 | async-start | bytes 524288 | tf_op jit(solution)/shard_map/basis/all_to_all | solution.py:88
  42.7 1.0 dynamic-slice_add_fusion
  43.7 17.2 %all-to-all-done.2 = bf16[16,32,256]{2,1,0:T(8,128)(2,1)S(1)} async-done(((bf16[16,32,256]{2,1,0:T(8,128)(2,1)}), bf16[16,32,256]{2,1,0:T(8,128)(2,1)S(1)}, u32[]{:S(2)}, u32[]{:S(2)}) %all-to-all-start.2) | async-done | bytes 262176 | tf_op jit(solution)/shard_map/basis/all_to_all | solution.py:88
  61.0 4.2 %all_to_all.87 = bf16[2,512,256]{2,1,0:T(8,128)(2,1)S(1)} all-to-all(bf16[2,512,256]{2,1,0:T(8,128)(2,1)S(1)} %broadcast_in_dim.33), channel_id=1, replica_groups={{0,4},{8,12},{16,20},{24,28},{32,36},{40,44},{48,52},{56,60},{64,68},{7..., dimensions={0} | all-to-all | bytes 1048576 | tf_op jit(solution)/shard_map/basis/all_to_all | solution.py:88
  66.7 9.6 %all_to_all.88 = f32[4,32,512]{2,1,0:T(8,128)S(1)} all-to-all(f32[4,32,512]{2,1,0:T(8,128)S(1)} %fusion.2), channel_id=1, replica_groups=mesh['dp'=4,'fsdp'=32,'tensor'=4] {'dp'}, dimensions={0} | all-to-all | bytes 524288 | tf_op jit(solution)/shard_map/left/all_to_all | solution.py:88
  76.4 10.9 %all_to_all.89 = f32[4,32,512]{2,1,0:T(8,128)S(1)} all-to-all(f32[4,32,512]{2,1,0:T(8,128)S(1)} %broadcast_in_dim.34), channel_id=1, replica_groups=mesh['dp'=4,'fsdp'=32,'tensor'=4] {'tensor'}, dimensions={0} | all-to-all | bytes 524288 | tf_op jit(solution)/shard_map/left/all_to_all | solution.py:88
  87.4 0.7 broadcast_in_dim.35
  88.1 4.8 %all-to-all-start.6 = ((f32[4,32,512]{2,1,0:T(8,128)}), f32[4,32,512]{2,1,0:T(8,128)S(1)}, u32[]{:S(2)}, u32[]{:S(2)}) async-start(f32[4,32,512]{2,1,0:T(8,128)} %broadcast_in_dim.35), calls=%async_computation.6 | async-start | bytes 524288 | tf_op jit(solution)/shard_map/left/all_to_all | solution.py:88
  92.9 5.2 %all-to-all-done.6 = f32[4,32,512]{2,1,0:T(8,128)S(1)} async-done(((f32[4,32,512]{2,1,0:T(8,128)}), f32[4,32,512]{2,1,0:T(8,128)S(1)}, u32[]{:S(2)}, u32[]{:S(2)}) %all-to-all-start.6) | async-done | bytes 262176 | tf_op jit(solution)/shard_map/left/all_to_all | solution.py:88
  98.2 1.0 convolution_bitcast_fusion
  99.2 3.8 %all_to_all.90 = f32[2,16,512]{2,1,0:T(8,128)S(1)} all-to-all(f32[2,16,512]{2,1,0:T(8,128)S(1)} %bitcast.63), channel_id=1, replica_groups={{0,4},{8,12},{16,20},{24,28},{32,36},{40,44},{48,52},{56,60},{64,68},{7..., dimensions={0} | all-to-all | bytes 131072 | tf_op jit(solution)/shard_map/gram/all_to_all | solution.py:88
  103.0 0.7 broadcast_in_dim.36
  103.7 4.1 %all-to-all-start.9 = ((f32[4,16,512]{2,1,0:T(8,128)}), f32[4,16,512]{2,1,0:T(8,128)S(1)}, u32[]{:S(2)}, u32[]{:S(2)}) async-start(f32[4,16,512]{2,1,0:T(8,128)} %broadcast_in_dim.36), calls=%async_computation.9 | async-start | bytes 262144 | tf_op jit(solution)/shard_map/gram/all_to_all | solution.py:88
  107.9 2.0 convolution_bitcast_fusion.1
  109.9 4.1 %all-to-all-done.9 = f32[4,16,512]{2,1,0:T(8,128)S(1)} async-done(((f32[4,16,512]{2,1,0:T(8,128)}), f32[4,16,512]{2,1,0:T(8,128)S(1)}, u32[]{:S(2)}, u32[]{:S(2)}) %all-to-all-start.9) | async-done | bytes 131104 | tf_op jit(solution)/shard_map/gram/all_to_all | solution.py:88
  114.0 3.6 %all-to-all-start.7 = ((f32[2,512,256]{2,1,0:T(8,128)}), f32[2,512,256]{2,1,0:T(8,128)S(1)}, u32[]{:S(2)}, u32[]{:S(2)}) async-start(f32[2,512,256]{2,1,0:T(8,128)} %convolution_bitcast_fusion.1), calls=%async_computation.7 | async-start | bytes 2097152 | tf_op jit(solution)/shard_map/product/all_to_all | solution.py:88
  117.6 2.1 all-to-all-done.7
  120.4 4.9 %all-to-all-start.10 = ((f32[4,16,512]{2,1,0:T(8,128)}), f32[4,16,512]{2,1,0:T(8,128)S(1)}, u32[]{:S(2)}, u32[]{:S(2)}) async-start(f32[4,16,512]{2,1,0:T(8,128)} %broadcast_in_dim.37), calls=%async_computation.10 | async-start | bytes 262144 | tf_op jit(solution)/shard_map/gram/all_to_all | solution.py:88
  125.3 0.9 reduce_sum.84
  126.2 14.5 %all-to-all-done.10 = f32[4,16,512]{2,1,0:T(8,128)S(1)} async-done(((f32[4,16,512]{2,1,0:T(8,128)}), f32[4,16,512]{2,1,0:T(8,128)S(1)}, u32[]{:S(2)}, u32[]{:S(2)}) %all-to-all-start.10) | async-done | bytes 131104 | tf_op jit(solution)/shard_map/gram/all_to_all | solution.py:88
  140.7 3.8 %all_to_all.91 = f32[2,16,512]{2,1,0:T(8,128)S(1)} all-to-all(f32[2,16,512]{2,1,0:T(8,128)S(1)} %broadcast_in_dim.38), channel_id=1, replica_groups={{0,4},{8,12},{16,20},{24,28},{32,36},{40,44},{48,52},{56,60},{64,68},{7..., dimensions={0} | all-to-all | bytes 131072 | tf_op jit(solution)/shard_map/gram/all_to_all | solution.py:88
  144.5 1.1 broadcast_in_dim.40
  145.6 4.9 %all-to-all-start.12 = ((f32[16,32,512]{2,1,0:T(8,128)}), f32[16,32,512]{2,1,0:T(8,128)S(1)}, u32[]{:S(2)}, u32[]{:S(2)}) async-start(f32[16,32,512]{2,1,0:T(8,128)} %broadcast_in_dim.40), calls=%async_computation.12 | async-start | bytes 2097152 | tf_op jit(solution)/shard_map/gram/all_to_all | solution.py:88
  150.5 46.6 %reduce-scatter.4.cloned.1.call-done = f32[32,256]{1,0:T(8,128)} async-done(((f32[512,256]{1,0:T(8,128)}), f32[32,256]{1,0:T(8,128)}) %reduce-scatter.4.cloned.1.call-update) | async-done | bytes 32784
  197.1 0.9 copy.68
  198.0 20.5 %inverse_factor.1 = f32[512,512]{1,0:T(8,128)S(1)} custom-call(f32[512,512]{1,0:T(8,128)S(1)} %bitcast.47), custom_call_target="tpu_custom_call" | custom-call | flops 20000000000 | bytes 2097152 | tf_op jit(solution)/shard_map/factor/inverse_factor/pallas_call | solution.py:71
  218.5 30.3 %all_gather.3 = f32[512,256]{1,0:T(8,128)S(1)} all-gather(f32[32,256]{1,0:T(8,128)S(1)} %copy.55), channel_id=1, replica_groups={{0,8,16,24,32,40,48,56,64,72,80,88,96,104,112,120},{4,12,20,28,36,44,52..., dimensions={0}, use_global_device_ids=true | all-gather | bytes 557056 | tf_op jit(solution)/shard_map/right/all_gather | solution.py:144
  249.2 4.6 %all_to_all.92 = f32[2,512,256]{1,2,0:T(8,128)S(1)} all-to-all(f32[2,512,256]{1,2,0:T(8,128)S(1)} %broadcast_in_dim.41), channel_id=1, replica_groups={{0,4},{8,12},{16,20},{24,28},{32,36},{40,44},{48,52},{56,60},{64,68},{7..., dimensions={0} | all-to-all | bytes 2097152 | tf_op jit(solution)/shard_map/right/all_to_all | solution.py:88
  253.8 1.9 multiply_reduce_fusion
  256.4 7.1 %all-to-all-start.15 = ((f32[16,1,512]{2,1,0:T(1,128)}), f32[16,1,512]{2,1,0:T(1,128)S(1)}, u32[]{:S(2)}, u32[]{:S(2)}) async-start(f32[16,1,512]{2,1,0:T(1,128)} %broadcast_in_dim.43), calls=%async_computation.15 | async-start | bytes 65536 | tf_op jit(solution)/shard_map/norms/all_to_all | solution.py:88
  263.4 1.2 fusion.3
  264.6 5.1 %all-to-all-done.15 = f32[16,1,512]{2,1,0:T(1,128)S(1)} async-done(((f32[16,1,512]{2,1,0:T(1,128)}), f32[16,1,512]{2,1,0:T(1,128)S(1)}, u32[]{:S(2)}, u32[]{:S(2)}) %all-to-all-start.15) | async-done | bytes 32800 | tf_op jit(solution)/shard_map/norms/all_to_all | solution.py:88
  269.9 0.7 fusion.1
  270.6 0.9 broadcast_in_dim.44
  271.5 4.9 %all-to-all-start.16 = ((bf16[4,144,512]{2,1,0:T(8,128)(2,1)}), bf16[4,144,512]{2,1,0:T(8,128)(2,1)S(1)}, u32[]{:S(2)}, u32[]{:S(2)}) async-start(bf16[4,144,512]{2,1,0:T(8,128)(2,1)} %broadcast_in_dim.44), calls=%async_computation.16 | async-start | bytes 1179648 | tf_op jit(solution)/shard_map/outputs/all_to_all | solution.py:88
  276.4 0.7 fusion
  277.1 7.2 %all-to-all-done.16 = bf16[4,144,512]{2,1,0:T(8,128)(2,1)S(1)} async-done(((bf16[4,144,512]{2,1,0:T(8,128)(2,1)}), bf16[4,144,512]{2,1,0:T(8,128)(2,1)S(1)}, u32[]{:S(2)}, u32[]{:S(2)}) %all-to-all-start.16) | async-done | bytes 589856 | tf_op jit(solution)/shard_map/outputs/all_to_all | solution.py:88
  284.3 1.1 broadcast_in_dim.42
  285.4 4.9 %all-to-all-start.14 = ((f32[4,128,512]{2,1,0:T(8,128)}), f32[4,128,512]{2,1,0:T(8,128)S(1)}, u32[]{:S(2)}, u32[]{:S(2)}) async-start(f32[4,128,512]{2,1,0:T(8,128)} %broadcast_in_dim.42), calls=%async_computation.14 | async-start | bytes 2097152 | tf_op jit(solution)/shard_map/outputs/all_to_all | solution.py:88
  291.0 1.0 copy.62
  292.0 0.8 copy.66
  292.9 9.1 %all-to-all-done.14 = f32[4,128,512]{2,1,0:T(8,128)S(1)} async-done(((f32[4,128,512]{2,1,0:T(8,128)}), f32[4,128,512]{2,1,0:T(8,128)S(1)}, u32[]{:S(2)}, u32[]{:S(2)}) %all-to-all-start.14) | async-done | bytes 1048608 | tf_op jit(solution)/shard_map/outputs/all_to_all | solution.py:88
  302.2 1.3 copy.61
  (37 shorter events, 5.6 us)
Async XLA Ops:
  7.2 0.8 copy-start
  8.6 4.8 %all-to-all-start.1 = ((bf16[2,16,256]{2,1,0:T(8,128)(2,1)}), bf16[2,16,256]{2,1,0:T(8,128)(2,1)S(1)}, u32[]{:S(2)}, u32[]{:S(2)}) async-start(bf16[2,16,256]{2,1,0:T(8,128)(2,1)} %copy.50), calls=%async_computation.1 | async-start | bytes 32768 | tf_op jit(solution)/shard_map/basis/all_to_all | solution.py:88
  31.4 29.6 %all-to-all-start.2 = ((bf16[16,32,256]{2,1,0:T(8,128)(2,1)}), bf16[16,32,256]{2,1,0:T(8,128)(2,1)S(1)}, u32[]{:S(2)}, u32[]{:S(2)}) async-start(bf16[16,32,256]{2,1,0:T(8,128)(2,1)} %broadcast_in_dim.31), calls=%async_computation.2 | async-start | bytes 524288 | tf_op jit(solution)/shard_map/basis/all_to_all | solution.py:88
  88.1 10.1 %all-to-all-start.6 = ((f32[4,32,512]{2,1,0:T(8,128)}), f32[4,32,512]{2,1,0:T(8,128)S(1)}, u32[]{:S(2)}, u32[]{:S(2)}) async-start(f32[4,32,512]{2,1,0:T(8,128)} %broadcast_in_dim.35), calls=%async_computation.6 | async-start | bytes 524288 | tf_op jit(solution)/shard_map/left/all_to_all | solution.py:88
  103.7 10.3 %all-to-all-start.9 = ((f32[4,16,512]{2,1,0:T(8,128)}), f32[4,16,512]{2,1,0:T(8,128)S(1)}, u32[]{:S(2)}, u32[]{:S(2)}) async-start(f32[4,16,512]{2,1,0:T(8,128)} %broadcast_in_dim.36), calls=%async_computation.9 | async-start | bytes 262144 | tf_op jit(solution)/shard_map/gram/all_to_all | solution.py:88
  114.0 5.7 %all-to-all-start.7 = ((f32[2,512,256]{2,1,0:T(8,128)}), f32[2,512,256]{2,1,0:T(8,128)S(1)}, u32[]{:S(2)}, u32[]{:S(2)}) async-start(f32[2,512,256]{2,1,0:T(8,128)} %convolution_bitcast_fusion.1), calls=%async_computation.7 | async-start | bytes 2097152 | tf_op jit(solution)/shard_map/product/all_to_all | solution.py:88
  120.4 20.3 %all-to-all-start.10 = ((f32[4,16,512]{2,1,0:T(8,128)}), f32[4,16,512]{2,1,0:T(8,128)S(1)}, u32[]{:S(2)}, u32[]{:S(2)}) async-start(f32[4,16,512]{2,1,0:T(8,128)} %broadcast_in_dim.37), calls=%async_computation.10 | async-start | bytes 262144 | tf_op jit(solution)/shard_map/gram/all_to_all | solution.py:88
  125.3 71.9 %reduce-scatter.4.cloned.1.call-start = ((), (), s32[]{:S(2)}) async-start(), calls=%async_computation.18 | async-start | bytes 557056
  145.6 52.4 %all-to-all-start.12 = ((f32[16,32,512]{2,1,0:T(8,128)}), f32[16,32,512]{2,1,0:T(8,128)S(1)}, u32[]{:S(2)}, u32[]{:S(2)}) async-start(f32[16,32,512]{2,1,0:T(8,128)} %broadcast_in_dim.40), calls=%async_computation.12 | async-start | bytes 2097152 | tf_op jit(solution)/shard_map/gram/all_to_all | solution.py:88
  256.4 13.3 %all-to-all-start.15 = ((f32[16,1,512]{2,1,0:T(1,128)}), f32[16,1,512]{2,1,0:T(1,128)S(1)}, u32[]{:S(2)}, u32[]{:S(2)}) async-start(f32[16,1,512]{2,1,0:T(1,128)} %broadcast_in_dim.43), calls=%async_computation.15 | async-start | bytes 65536 | tf_op jit(solution)/shard_map/norms/all_to_all | solution.py:88
  271.5 12.8 %all-to-all-start.16 = ((bf16[4,144,512]{2,1,0:T(8,128)(2,1)}), bf16[4,144,512]{2,1,0:T(8,128)(2,1)S(1)}, u32[]{:S(2)}, u32[]{:S(2)}) async-start(bf16[4,144,512]{2,1,0:T(8,128)(2,1)} %broadcast_in_dim.44), calls=%async_computation.16 | async-start | bytes 1179648 | tf_op jit(solution)/shard_map/outputs/all_to_all | solution.py:88
  285.4 16.5 %all-to-all-start.14 = ((f32[4,128,512]{2,1,0:T(8,128)}), f32[4,128,512]{2,1,0:T(8,128)S(1)}, u32[]{:S(2)}, u32[]{:S(2)}) async-start(f32[4,128,512]{2,1,0:T(8,128)} %broadcast_in_dim.42), calls=%async_computation.14 | async-start | bytes 2097152 | tf_op jit(solution)/shard_map/outputs/all_to_all | solution.py:88
Sparse Core Ops, SparseCore 0:
  129.5 67.6 reduce-scatter.3

commit v2 on v1

v2 whole, which is shorter than its diff:
```python
import functools
import math

import jax
import jax.numpy as jnp
from jax import lax
from jax.experimental import pallas as pl
from jax.experimental.pallas import tpu as pltpu
from jax.sharding import Mesh
from jax.sharding import PartitionSpec as P

HIGH = lax.Precision.HIGHEST
EDGE = 128
VMEM = pl.BlockSpec(memory_space=pltpu.VMEM)
SMEM = pl.BlockSpec(memory_space=pltpu.SMEM)


def dot(a, b, dims):
    return lax.dot_general(a, b, (dims, ((), ())), precision=HIGH, preferred_element_type=jnp.float32)


def call(kernel, shapes, args, flops, scratch=(), scalars=0, dtype=jnp.float32):
    dtypes = dtype if isinstance(dtype, tuple) else (dtype,) * len(shapes)
    return pl.pallas_call(
        kernel,
        out_shape=[jax.ShapeDtypeStruct(s, t) for s, t in zip(shapes, dtypes)],
        in_specs=[SMEM] * scalars + [VMEM] * (len(args) - scalars),
        out_specs=[VMEM] * len(shapes),
        scratch_shapes=[pltpu.VMEM(shape, jnp.float32) for shape in scratch],
        compiler_params=pltpu.CompilerParams(vmem_limit_bytes=32 * 1024 * 1024),
        cost_estimate=pl.CostEstimate(flops=flops, bytes_accessed=4 * 1024 * 1024, transcendentals=0),
        name=kernel.func.__name__ if isinstance(kernel, functools.partial) else kernel.__name__,
    )(*args)


def invert_block(block):
    size = block.shape[0]
    steps = size // 8
    sub = lax.broadcasted_iota(jnp.int32, (8, size), 0)
    lane = lax.broadcasted_iota(jnp.int32, (8, size), 1)
    full = (8, size)
    rows = [block[8 * i : 8 * i + 8] for i in range(steps)]
    done = []
    for k in range(steps):
        here = (lane >= 8 * k) & (lane < 8 * k + 8)
        columns = [[jnp.broadcast_to(r[:, 8 * k + m : 8 * k + m + 1], full) for m in range(8)] for r in rows[k:]]
        cur = jnp.where(here, (lane - 8 * k == sub).astype(jnp.float32), rows[k])
        col = columns[0]
        result = jnp.zeros(full, jnp.float32)
        for j in range(8):
            at = sub == j
            pivot = jnp.broadcast_to(col[j][j : j + 1], full)
            row = jnp.broadcast_to(cur[j : j + 1], full)
            result = jnp.where(at, row * lax.rsqrt(pivot), result)
            recip = 1.0 / pivot
            mult = jnp.where(at, -1.0, col[j])
            cur = jnp.where(at, 0.0, cur) - (mult * row) * recip
            for m in range(j + 1, 8):
                lead = jnp.broadcast_to(col[m][j : j + 1], full)
                col[m] = jnp.where(at, 0.0, col[m]) - (mult * lead) * recip
        done.append(jnp.where(lane <= 8 * k + sub, result, 0.0))
        if k + 1 < steps:
            spread = [jnp.broadcast_to(cur[m : m + 1], full) for m in range(8)]
            for i in range(k + 1, steps):
                acc = jnp.where(here, 0.0, rows[i])
                for m in range(8):
                    acc = acc - columns[i - k][m] * spread[m]
                rows[i] = acc
    return jnp.concatenate(done, axis=0)


def eliminate(work, out, first, last, base):
    size = work.shape[1]
    for k in range(first, last):
        a, b = k * EDGE, (k + 1) * EDGE
        low, high = a - base, b - base
        inv = invert_block(work[low:high, a:b])
        if k:
            out[low:high, :a] = dot(inv, work[low:high, :a], ((1,), (0,)))
        out[low:high, a:b] = inv
        if b < size:
            out[low:high, b:] = jnp.zeros((EDGE, size - b), jnp.float32)
            upper = dot(inv, work[low:high, b:], ((1,), (0,)))
            full = jnp.concatenate([out[low:high, :b], upper], axis=1)
            work[high:, a:b] = jnp.zeros((size - b, EDGE), jnp.float32)
            work[high:, :] -= dot(upper, full, ((0,), (0,)))


def upper_blocks(count):
    return [(k, j) for k in range(count) for j in range(k, count)]


def factor_top(gram_ref, top_ref, rest_ref, work):
    size = work.shape[0]
    count = size // EDGE
    work[...] = jnp.zeros_like(work)
    for at, (k, j) in enumerate(upper_blocks(count)):
        work[k * EDGE : (k + 1) * EDGE, j * EDGE : (j + 1) * EDGE] = gram_ref[at * EDGE : (at + 1) * EDGE, :]
    eliminate(work, top_ref, 0, count // 2, 0)
    rest_ref[...] = work[size // 2 :, :]


def factor_rest(rest_ref, top_ref, left_ref, low_ref, basis_ref, work):
    size = work.shape[1]
    half = size // 2
    count = size // EDGE
    work[...] = rest_ref[...]
    eliminate(work, low_ref, count // 2, count, half)
    basis_ref[:, :half] = dot(left_ref[:, :half], top_ref[:, :half], ((1,), (1,)))
    basis_ref[:, half:] = dot(left_ref[...], low_ref[...], ((1,), (1,)))


def products(near, far, place_ref, left_ref, total_ref, out_ref, gram):
    left = left_ref[...]
    rank = left.shape[1]
    cols = total_ref.shape[1]
    blocks = cols // EDGE
    piece = rank // (2 * near * far)
    prod = dot(left, total_ref[...], ((0,), (0,)))
    for i in range(2 * near * far):
        to, rest = divmod(i, near * far)
        for j in range(blocks):
            at = (rest * blocks + j) * piece
            out_ref[to, at : at + piece, :] = prod[i * piece : (i + 1) * piece, j * EDGE : (j + 1) * EDGE]
    at = 0
    for k in range(rank // EDGE):
        row = dot(left[:, k * EDGE : (k + 1) * EDGE], left[:, k * EDGE :], ((0,), (0,)))
        for j in range(row.shape[1] // EDGE):
            gram[at : at + EDGE, :] = row[:, j * EDGE : (j + 1) * EDGE]
            at += EDGE
    begin = near * far * blocks * piece
    slot = out_ref.shape[1] - begin
    for to in range(2):
        out_ref[to, begin:, :] = gram[pl.ds(pl.multiple_of((2 * place_ref[0] + to) * slot, 8), slot), :]


def finish(prod_ref, top_ref, low_ref, right_ref, squares_ref, prod):
    half = top_ref.shape[0]
    for j in range(prod_ref.shape[1]):
        prod[:, j * EDGE : (j + 1) * EDGE] = prod_ref[:, j].reshape(2 * half, EDGE)
    top = dot(top_ref[:, :half], prod[:half, :], ((1,), (0,)))
    low = dot(low_ref[...], prod[...], ((1,), (0,)))
    right_ref[:half, :] = top
    right_ref[half:, :] = low
    ones = jnp.ones((8, prod.shape[1]), jnp.float32)
    squares_ref[:, :half] = dot(ones, top * top, ((1,), (1,)))
    squares_ref[:, half:] = dot(ones, low * low, ((1,), (1,)))


def outputs(scale, me_ref, squares_ref, basis_ref, right_ref, out_ref):
    rows, rank = basis_ref.shape
    own = out_ref.shape[1] - 2 * rows
    norms = lax.rsqrt(jnp.sum(squares_ref[...], axis=0, keepdims=True) + 1e-06)
    basis = basis_ref[...]
    row = lax.broadcasted_iota(jnp.int32, (own, rank), 0)
    lane = lax.broadcasted_iota(jnp.int32, (own, rank), 1)
    pick = jnp.where(lane == row + me_ref[0] * own, norms, 0.0)
    mixed = dot(jnp.concatenate([0.05 * basis, basis * (scale * norms), pick], axis=0), right_ref[...], ((1,), (0,)))
    mixed = mixed.astype(out_ref.dtype)
    for to in range(out_ref.shape[0]):
        out_ref[to] = mixed


def merge(d_ref, mixed_ref, *refs):
    totals, (momentum_ref, update_ref, basis_ref) = refs[:-3], refs[-3:]
    n = len(totals)
    rows, cols = totals[0].shape
    for k in range(n):
        q = lax.rem(d_ref[0] + (n - k), n)
        at = pl.ds(pl.multiple_of(q * cols, cols), cols)
        momentum_ref[:, at] = totals[k][...] - mixed_ref[q, :rows, :].astype(jnp.float32)
    for q in range(n):
        update_ref[:, q * cols : (q + 1) * cols] = mixed_ref[q, rows : 2 * rows, :]
        basis_ref[:, q * cols : (q + 1) * cols] = mixed_ref[q, 2 * rows :, :]


def swap(x, axis):
    return lax.all_to_all(x, axis, 0, 0, tiled=True)


def share(x, axis):
    return swap(jnp.broadcast_to(x[None], (lax.axis_size(axis),) + x.shape), axis)


def per_device(momentum, grads, right_basis):
    rows, local_cols = momentum.shape
    n_dp, n_far, n_near, n_tensor = (lax.axis_size(a) for a in ("dp", "far", "near", "tensor"))
    n_slots = 2 * n_dp * n_tensor
    rank_local = right_basis.shape[1]
    n_fsdp = 2 * n_far * n_near
    rank = rank_local * n_fsdp
    cols = local_cols // n_dp
    factor_scale = math.sqrt(rows * n_fsdp * local_cols * n_tensor / rank)
    d = lax.axis_index("dp")
    me = lax.axis_index(("far", "near", "core")).reshape(1)
    place = lax.axis_index(("dp", "tensor")).reshape(1)
    slot = len(upper_blocks(rank // EDGE)) * EDGE // n_slots

    def turn(k):
        return [(i, (i + k) % n_dp) for i in range(n_dp)]

    with jax.named_scope("basis"):
        mine = lax.dynamic_slice_in_dim(right_basis.T, d * cols, cols, 1)
        part = share(mine, ("far", "near"))
        basis_t = share(part, "core").transpose(1, 0, 2, 3).reshape(rank, cols)
    with jax.named_scope("total"):
        def column(x, k):
            return lax.dynamic_slice_in_dim(x, (d + k) % n_dp * cols, cols, 1)

        blocks = [lax.ppermute(column(grads[0], k), "dp", turn(k)) for k in range(1, n_dp)]
        total = sum((b.astype(jnp.float32) for b in blocks), column(grads[0], 0).astype(jnp.float32))
        total = column(momentum, 0) + total
    with jax.named_scope("left"):
        partial = dot(total, basis_t.astype(jnp.float32), ((1,), (1,)))
        partial = jnp.sum(swap(partial.reshape(n_dp, rows // n_dp, rank), "dp"), axis=0)
        partial = share(partial, ("dp", "tensor")).reshape(n_dp, n_tensor, rows // n_dp, rank)
        left = jnp.sum(partial, axis=1).reshape(rows, rank)
    with jax.named_scope("totals"):
        totals = [total] + [lax.ppermute(total, "dp", turn(k)) for k in range(1, n_dp)]
    with jax.named_scope("products"):
        prod_rows = rank * cols // EDGE // 2
        both = call(
            functools.partial(products, n_near, n_far),
            [(2, prod_rows + slot, EDGE)],
            (place, left, total),
            10**9,
            [(n_slots * slot, EDGE)],
            1,
        )[0]
        both = jnp.sum(swap(both, "core"), axis=0)
        for axis, n in (("near", n_near), ("far", n_far)):
            prod_rows = both.shape[0] - slot
            prod = both[:prod_rows].reshape(n, prod_rows // n, EDGE)
            gram = jnp.broadcast_to(both[prod_rows:][None], (n, slot, EDGE))
            both = swap(jnp.concatenate([prod, gram], axis=1), axis)
            if axis == "near":
                both, totals[1], totals[3] = lax.optimization_barrier((both, totals[1], totals[3]))
            else:
                both, totals[2] = lax.optimization_barrier((both, totals[2]))
            both = jnp.sum(both, axis=0)
        prod, gram = both[:-slot], both[-slot:]
        gram = share(gram, ("dp", "tensor", "core")).reshape(n_slots * slot, EDGE)
        prod, gram = lax.optimization_barrier((prod, gram))
    with jax.named_scope("factor"):
        half = (rank // 2, rank)
        top, rest = call(factor_top, [half, half], (gram,), 10**10, [(rank, rank)])
        prod = share(prod, "far")
        prod, rest = lax.optimization_barrier((prod, rest))
        low, left_basis = call(factor_rest, [half, (rows, rank)], (rest, top, left), 10**10, [half])
        prod = share(prod, "near")
        prod, low = lax.optimization_barrier((prod, low))
    with jax.named_scope("right"):
        prod = share(prod, "core").reshape(n_fsdp, cols // EDGE, rank_local, EDGE)
        right_t, squares = call(
            finish, [(rank, cols), (8, rank)], (prod, top, low), 2 * 10**9, [(rank, cols)]
        )
    with jax.named_scope("norms"):
        squares = share(squares[:1], ("dp", "tensor")).reshape(n_dp * n_tensor, rank)
    with jax.named_scope("outputs"):
        mixed = call(
            functools.partial(outputs, factor_scale),
            [(n_dp, 2 * rows + rank_local, cols)],
            (me, squares, left_basis, right_t),
            10**9,
            (),
            1,
            jnp.bfloat16,
        )[0]
        mixed = swap(mixed, "dp")
        new_momentum, update, basis = call(
            merge,
            [(rows, local_cols), (rows, local_cols), (rank_local, local_cols)],
            (d.reshape(1), mixed, *totals),
            10**6,
            (),
            1,
            (jnp.float32, jnp.bfloat16, jnp.bfloat16),
        )
    return (new_momentum, update, basis.T)


def solution(mesh):
    n_dp, n_fsdp, n_tensor = (mesh.shape[a] for a in ("dp", "fsdp", "tensor"))
    near = 4
    far = n_fsdp // 2 // near
    fine = Mesh(mesh.devices.reshape(n_dp, far, near, 2, n_tensor), ("dp", "far", "near", "core", "tensor"))
    fsdp = ("far", "near", "core")
    in_specs = (P(fsdp, "tensor"), P("dp", fsdp, "tensor"), P("tensor", fsdp))
    out_specs = (P(fsdp, "tensor"), P(fsdp, "tensor"), P("tensor", fsdp))
    return jax.shard_map(
        per_device, mesh=fine, in_specs=in_specs, out_specs=out_specs, check_vma=False
    )
```

time: 312 us -> 225 us (0.72)
  waiting for transfers between devices: 111 us -> 66.9 us
  blocking collectives: 84.5 us -> 41.2 us
  starting transfers between devices: 53.7 us -> 75.4 us
  between operations: 14.3 us -> 0.99 us
  local copies, waits for them, and re-layouts: 15.9 us -> 7.88 us
  matrix products: 8.22 us -> 0.65 us
  Pallas kernels: 20.5 us -> 27.6 us
    unnamed x2 -> x0, waiting for transfers between devices: 46.6 us -> none
    all_gather x1 -> x0, blocking collectives: 30.3 us -> none  [per_device(): lax.all_gather(prod, 'fsdp', axis=0, tiled=True, axis_index_groups=zs)]
    ppermute x0 -> x6, starting transfers between devices: none -> 19.7 us  [the longest x3 9.88 us: per_device(): lax.ppermute(column(grads[0], k), 'dp', turn(k))]
    ppermute x0 -> x6, waiting for transfers between devices: none -> 18.7 us  [the longest x3 14.4 us: per_device(): lax.ppermute(total, 'dp', turn(k))]
    all_to_all x10 -> x8, waiting for transfers between devices: 64.4 us -> 48.2 us  [swap(): return lax.all_to_all(x, axis, 0, 0, tiled=True)]
    all_to_all x7 -> x5, blocking collectives: 54.1 us -> 41.2 us  [swap(): return lax.all_to_all(x, axis, 0, 0, tiled=True)]
    dot_general x7 -> x1, matrix products: 8.22 us -> 0.65 us  [dot(): lax.dot_general(a, b, (dims, ((), ())), precision=HIGH, preferred_element...]
    pallas_call x1 -> x6, Pallas kernels: 20.5 us -> 27.6 us  [call(): pl.pallas_call(kernel, out_shape=[jax.ShapeDtypeStruct(s, t) for s, t in...]
  transfers between devices with their start and end apart: 11 -> 14, of which waited for: 9 -> 13; matrix products, arithmetic and copies ran while one was open for 4% -> 0% of each run, Pallas kernels for 0% -> 10%
where the time goes in v2:
time: 225 us; the launch traced here: 224 us
  starting transfers between devices  75.4 us (34%)
  waiting for transfers between devices  66.9 us (30%)
  blocking collectives  41.2 us (18%)
  Pallas kernels  27.6 us (12%)
  local copies, waits for them, and re-layouts  7.88 us (4%)
  other arithmetic  2.85 us (1%)
    all_to_all x8, starting transfers between devices, swap(): return lax.all_to_all(x, axis, 0, 0, tiled=True)  55.8 us
    all_to_all x8, waiting for transfers between devices, swap(): return lax.all_to_all(x, axis, 0, 0, tiled=True)  48.2 us
    all_to_all x5, blocking collectives, swap(): return lax.all_to_all(x, axis, 0, 0, tiled=True)  41.2 us
    pallas_call x6, Pallas kernels, call(): pl.pallas_call(kernel, out_shape=[jax.ShapeDtypeStruct(s, t) for s, t in...  27.6 us
    ppermute x3, waiting for transfers between devices, per_device(): lax.ppermute(total, 'dp', turn(k))  14.4 us
    ppermute x3, starting transfers between devices, per_device(): lax.ppermute(column(grads[0], k), 'dp', turn(k))  9.88 us
    ppermute x3, starting transfers between devices, per_device(): lax.ppermute(total, 'dp', turn(k))  9.8 us
    broadcast_in_dim x8, local copies, waits for them, and re-layouts, share(): jnp.broadcast_to(x[None], (lax.axis_size(axis),) + x.shape)  6.1 us
  transfers between devices with their start and end apart: 14, of which 13 were waited for; matrix products, arithmetic and copies ran while one was open for 0% of the time, Pallas kernels for 10%

profile of v2, /device:TPU:2, one launch (start us, length us, event | category | flops | bytes accessed | tf_op | source)
XLA Modules:
  0.0 223.5 jit_solution(16908418462525023288)
XLA Ops:
  0.7 0.8 copy-done
  1.5 0.7 broadcast_in_dim.22
  2.2 15.2 %all-to-all-start = ((bf16[16,16,512]{2,1,0:T(8,128)(2,1)}), bf16[16,16,512]{2,1,0:T(8,128)(2,1)S(1)}, u32[]{:S(2)}, u32[]{:S(2)}) async-start(bf16[16,16,512]{2,1,0:T(8,128)(2,1)} %broadcast_in_dim.22), calls=%async_computation | async-start | bytes 524288 | tf_op jit(solution)/shard_map/basis/all_to_all | solution.py:178
  17.5 3.4 %collective-permute-start = (bf16[128,512]{1,0:T(8,128)(2,1)S(1)}, bf16[128,512]{1,0:T(8,128)(2,1)S(1)}, u32[]{:S(2)}, u32[]{:S(2)}) collective-permute-start(bf16[128,512]{1,0:T(8,128)(2,1)S(1)} %get-tuple-element.43), channel_id=1, source_target_pairs={{0,128},{128,256},{256,384},{384,0},{1,129},{129,257},{257,385},{3... | collective-permute-start | bytes 393224 | tf_op jit(solution)/shard_map/total/ppermute | solution.py:210
  20.9 2.4 %collective-permute-start.2 = (bf16[128,512]{1,0:T(8,128)(2,1)S(1)}, bf16[128,512]{1,0:T(8,128)(2,1)S(1)}, u32[]{:S(2)}, u32[]{:S(2)}) collective-permute-start(bf16[128,512]{1,0:T(8,128)(2,1)S(1)} %get-tuple-element.44), channel_id=1, source_target_pairs={{0,384},{128,0},{256,128},{384,256},{1,385},{129,1},{257,129},{385... | collective-permute-start | bytes 393224 | tf_op jit(solution)/shard_map/total/ppermute | solution.py:210
  23.4 4.0 %collective-permute-start.1 = (bf16[128,512]{1,0:T(8,128)(2,1)S(1)}, bf16[128,512]{1,0:T(8,128)(2,1)S(1)}, u32[]{:S(2)}, u32[]{:S(2)}) collective-permute-start(bf16[128,512]{1,0:T(8,128)(2,1)S(1)} %get-tuple-element.45), channel_id=1, source_target_pairs={{0,256},{128,384},{256,0},{384,128},{1,257},{129,385},{257,1},{385... | collective-permute-start | bytes 393224 | tf_op jit(solution)/shard_map/total/ppermute | solution.py:210
  27.8 4.0 %collective-permute-done.1 = bf16[128,512]{1,0:T(8,128)(2,1)S(1)} collective-permute-done((bf16[128,512]{1,0:T(8,128)(2,1)S(1)}, bf16[128,512]{1,0:T(8,128)(2,1)S(1)}, u32[]{:S(2)}, u32[]{:S(2)}) %collective-permute-start.1) | collective-permute-done | bytes 131104 | tf_op jit(solution)/shard_map/total/ppermute | solution.py:210
  31.7 1.0 fusion.2.total_ref.refs_0_
  32.8 3.0 %all-to-all-done = bf16[16,16,512]{2,1,0:T(8,128)(2,1)S(1)} async-done(((bf16[16,16,512]{2,1,0:T(8,128)(2,1)}), bf16[16,16,512]{2,1,0:T(8,128)(2,1)S(1)}, u32[]{:S(2)}, u32[]{:S(2)}) %all-to-all-start) | async-done | bytes 262176 | tf_op jit(solution)/shard_map/basis/all_to_all | solution.py:178
  35.8 4.2 %all_to_all.65 = bf16[2,16,16,512]{3,2,1,0:T(8,128)(2,1)S(1)} all-to-all(bf16[2,16,16,512]{3,2,1,0:T(8,128)(2,1)S(1)} %broadcast_in_dim.23), channel_id=1, replica_groups=mesh['dp'=4,'far'=4,'near'=4,'core'=2,'tensor'=4] {'core'}, dimensions={0} | all-to-all | bytes 1048576 | tf_op jit(solution)/shard_map/basis/all_to_all | solution.py:178
  40.7 10.1 %all_to_all.66 = f32[4,32,512]{2,1,0:T(8,128)S(1)} all-to-all(f32[4,32,512]{2,1,0:T(8,128)S(1)} %fusion.3), channel_id=1, replica_groups=mesh['dp'=4,'far'=4,'near'=4,'core'=2,'tensor'=4] {'dp'}, dimensions={0} | all-to-all | bytes 524288 | tf_op jit(solution)/shard_map/left/all_to_all | solution.py:178
  50.9 1.1 broadcast_in_dim.24
  52.0 6.5 %all-to-all-start.3 = ((f32[16,32,512]{2,1,0:T(8,128)}), f32[16,32,512]{2,1,0:T(8,128)S(1)}, u32[]{:S(2)}, u32[]{:S(2)}) async-start(f32[16,32,512]{2,1,0:T(8,128)} %broadcast_in_dim.24), calls=%async_computation.3 | async-start | bytes 2097152 | tf_op jit(solution)/shard_map/left/all_to_all | solution.py:178
  58.5 14.1 %all-to-all-done.3 = f32[16,32,512]{2,1,0:T(8,128)S(1)} async-done(((f32[16,32,512]{2,1,0:T(8,128)}), f32[16,32,512]{2,1,0:T(8,128)S(1)}, u32[]{:S(2)}, u32[]{:S(2)}) %all-to-all-start.3) | async-done | bytes 1048608 | tf_op jit(solution)/shard_map/left/all_to_all | solution.py:178
  72.7 1.5 products.1
  74.2 4.6 %all_to_all.67 = f32[2,1064,128]{2,1,0:T(8,128)S(1)} all-to-all(f32[2,1064,128]{2,1,0:T(8,128)S(1)} %products.1), channel_id=1, replica_groups=mesh['dp'=4,'far'=4,'near'=4,'core'=2,'tensor'=4] {'core'}, dimensions={0} | all-to-all | bytes 2179072 | tf_op jit(solution)/shard_map/products/all_to_all | solution.py:178
  79.0 0.9 pad_maximum_fusion
  79.9 4.4 %all-to-all-start.5 = ((f32[4,296,128]{2,1,0:T(8,128)}), f32[4,296,128]{2,1,0:T(8,128)S(1)}, u32[]{:S(2)}, u32[]{:S(2)}) async-start(f32[4,296,128]{2,1,0:T(8,128)} %pad_maximum_fusion), calls=%async_computation.5 | async-start | bytes 1212416 | tf_op jit(solution)/shard_map/products/all_to_all | solution.py:178
  84.2 3.9 %collective-permute-start.4 = (f32[128,512]{1,0:T(8,128)S(1)}, f32[128,512]{1,0:T(8,128)S(1)}, u32[]{:S(2)}, u32[]{:S(2)}) collective-permute-start(f32[128,512]{1,0:T(8,128)S(1)} %fusion.2.total_ref.refs_0_), channel_id=1, source_target_pairs={{0,384},{128,0},{256,128},{384,256},{1,385},{129,1},{257,129},{385... | collective-permute-start | bytes 786440 | tf_op jit(solution)/shard_map/totals/ppermute | solution.py:219
  88.1 2.0 collective-permute-start.3
  90.1 4.1 %collective-permute-done.4.refs_3_ = f32[128,512]{1,0:T(8,128)S(1)} collective-permute-done((f32[128,512]{1,0:T(8,128)S(1)}, f32[128,512]{1,0:T(8,128)S(1)}, u32[]{:S(2)}, u32[]{:S(2)}) %collective-permute-start.4) | collective-permute-done | bytes 262176 | tf_op jit(solution)/shard_map/totals/ppermute | solution.py:219
  94.2 3.6 %collective-permute-done.3.refs_1_ = f32[128,512]{1,0:T(8,128)S(1)} collective-permute-done((f32[128,512]{1,0:T(8,128)S(1)}, f32[128,512]{1,0:T(8,128)S(1)}, u32[]{:S(2)}, u32[]{:S(2)}) %collective-permute-start.3) | collective-permute-done | bytes 262176 | tf_op jit(solution)/shard_map/totals/ppermute | solution.py:219
  97.8 3.0 %all-to-all-done.5 = f32[4,296,128]{2,1,0:T(8,128)S(1)} async-done(((f32[4,296,128]{2,1,0:T(8,128)}), f32[4,296,128]{2,1,0:T(8,128)S(1)}, u32[]{:S(2)}, u32[]{:S(2)}) %all-to-all-start.5) | async-done | bytes 606240 | tf_op jit(solution)/shard_map/products/all_to_all | solution.py:178
  100.8 0.7 pad_maximum_fusion.1
  101.5 8.2 %all-to-all-start.6 = ((f32[4,104,128]{2,1,0:T(8,128)}), f32[4,104,128]{2,1,0:T(8,128)S(1)}, u32[]{:S(2)}, u32[]{:S(2)}) async-start(f32[4,104,128]{2,1,0:T(8,128)} %pad_maximum_fusion.1), calls=%async_computation.6 | async-start | bytes 425984 | tf_op jit(solution)/shard_map/products/all_to_all | solution.py:178
  109.8 4.0 %collective-permute-start.5 = (f32[128,512]{1,0:T(8,128)S(1)}, f32[128,512]{1,0:T(8,128)S(1)}, u32[]{:S(2)}, u32[]{:S(2)}) collective-permute-start(f32[128,512]{1,0:T(8,128)S(1)} %fusion.2.total_ref.refs_0_), channel_id=1, source_target_pairs={{0,256},{128,384},{256,0},{384,128},{1,257},{129,385},{257,1},{385... | collective-permute-start | bytes 786440 | tf_op jit(solution)/shard_map/totals/ppermute | solution.py:219
  113.8 6.6 %collective-permute-done.5.refs_2_ = f32[128,512]{1,0:T(8,128)S(1)} collective-permute-done((f32[128,512]{1,0:T(8,128)S(1)}, f32[128,512]{1,0:T(8,128)S(1)}, u32[]{:S(2)}, u32[]{:S(2)}) %collective-permute-start.5) | collective-permute-done | bytes 262176 | tf_op jit(solution)/shard_map/totals/ppermute | solution.py:219
  120.4 5.3 %all-to-all-done.6 = f32[4,104,128]{2,1,0:T(8,128)S(1)} async-done(((f32[4,104,128]{2,1,0:T(8,128)}), f32[4,104,128]{2,1,0:T(8,128)S(1)}, u32[]{:S(2)}, u32[]{:S(2)}) %all-to-all-start.6) | async-done | bytes 213024 | tf_op jit(solution)/shard_map/products/all_to_all | solution.py:178
  125.7 0.9 broadcast_in_dim.27
  126.6 5.6 %all-to-all-start.7 = ((f32[32,40,128]{2,1,0:T(8,128)}), f32[32,40,128]{2,1,0:T(8,128)S(1)}, u32[]{:S(2)}, u32[]{:S(2)}) async-start(f32[32,40,128]{2,1,0:T(8,128)} %broadcast_in_dim.27), calls=%async_computation.7 | async-start | bytes 1310720 | tf_op jit(solution)/shard_map/products/all_to_all | solution.py:178
  132.2 10.8 %all-to-all-done.7 = f32[32,40,128]{2,1,0:T(8,128)S(1)} async-done(((f32[32,40,128]{2,1,0:T(8,128)}), f32[32,40,128]{2,1,0:T(8,128)S(1)}, u32[]{:S(2)}, u32[]{:S(2)}) %all-to-all-start.7) | async-done | bytes 655392 | tf_op jit(solution)/shard_map/products/all_to_all | solution.py:178
  143.7 6.5 %all-to-all-start.8 = ((f32[4,64,128]{2,1,0:T(8,128)}), f32[4,64,128]{2,1,0:T(8,128)S(1)}, u32[]{:S(2)}, u32[]{:S(2)}) async-start(f32[4,64,128]{2,1,0:T(8,128)} %broadcast_in_dim.28), calls=%async_computation.8 | async-start | bytes 262144 | tf_op jit(solution)/shard_map/factor/all_to_all | solution.py:178
  150.2 10.7 %factor_top.1 = (f32[256,512]{1,0:T(8,128)S(1)}, f32[256,512]{1,0:T(8,128)S(1)}) custom-call(f32[1280,128]{1,0:T(8,128)S(1)} %bitcast.35), custom_call_target="tpu_custom_call" | custom-call | flops 10000000000 | bytes 4194304 | tf_op jit(solution)/shard_map/factor/factor_top/pallas_call | solution.py:24
  161.0 3.1 %all-to-all-done.8 = f32[4,64,128]{2,1,0:T(8,128)S(1)} async-done(((f32[4,64,128]{2,1,0:T(8,128)}), f32[4,64,128]{2,1,0:T(8,128)S(1)}, u32[]{:S(2)}, u32[]{:S(2)}) %all-to-all-start.8) | async-done | bytes 131104 | tf_op jit(solution)/shard_map/factor/all_to_all | solution.py:178
  164.1 0.8 broadcast_in_dim.29
  165.0 4.3 %all-to-all-start.9 = ((f32[4,4,64,128]{3,2,1,0:T(8,128)}), f32[4,4,64,128]{3,2,1,0:T(8,128)}, u32[]{:S(2)}, u32[]{:S(2)}) async-start(f32[4,4,64,128]{3,2,1,0:T(8,128)} %broadcast_in_dim.29), calls=%async_computation.9 | async-start | bytes 1048576 | tf_op jit(solution)/shard_map/factor/all_to_all | solution.py:178
  169.3 10.5 %factor_rest.1 = (f32[256,512]{1,0:T(8,128)S(1)}, f32[128,512]{1,0:T(8,128)S(1)}) custom-call(f32[256,512]{1,0:T(8,128)S(1)} %get-tuple-element.29.rest_ref, f32[256,512]{1,0:T(8,128)S(1)} %get-tuple-element.30.top_ref, f32[128,512]{1,0:T(8,128)S(1)} %bitcast.37), custom_call_target="tpu_custom_call" | custom-call | flops 10000000000 | bytes 4194304 | tf_op jit(solution)/shard_map/factor/factor_rest/pallas_call | solution.py:24
  179.8 0.8 copy-done.1
  180.6 2.6 %all-to-all-done.9 = f32[4,4,64,128]{3,2,1,0:T(8,128)} async-done(((f32[4,4,64,128]{3,2,1,0:T(8,128)}), f32[4,4,64,128]{3,2,1,0:T(8,128)}, u32[]{:S(2)}, u32[]{:S(2)}) %all-to-all-start.9) | async-done | bytes 524320 | tf_op jit(solution)/shard_map/factor/all_to_all | solution.py:178
  183.2 1.2 broadcast_in_dim.30
  184.4 4.7 %all_to_all.68 = f32[2,4,4,64,128]{4,3,2,1,0:T(8,128)S(1)} all-to-all(f32[2,4,4,64,128]{4,3,2,1,0:T(8,128)S(1)} %broadcast_in_dim.30), channel_id=1, replica_groups=mesh['dp'=4,'far'=4,'near'=4,'core'=2,'tensor'=4] {'core'}, dimensions={0} | all-to-all | bytes 2097152 | tf_op jit(solution)/shard_map/right/all_to_all | solution.py:178
  189.1 2.4 %finish.1 = (f32[512,512]{1,0:T(8,128)S(1)}, f32[8,512]{1,0:T(8,128)S(1)}) custom-call(f32[32,4,16,128]{3,2,1,0:T(8,128)S(1)} %bitcast.34, f32[256,512]{1,0:T(8,128)S(1)} %get-tuple-element.30.top_ref, f32[256,512]{1,0:T(8,128)S(1)} %copy-done.2), custom_call_target="tpu_custom_call" | custom-call | flops 2000000000 | bytes 4194304 | tf_op jit(solution)/shard_map/right/finish/pallas_call | solution.py:24
  191.5 0.7 broadcast_in_dim.32
  192.2 5.0 %all-to-all-start.11 = ((f32[16,1,512]{2,1,0:T(1,128)}), f32[16,1,512]{2,1,0:T(1,128)S(1)}, u32[]{:S(2)}, u32[]{:S(2)}) async-start(f32[16,1,512]{2,1,0:T(1,128)} %broadcast_in_dim.32), calls=%async_computation.11 | async-start | bytes 65536 | tf_op jit(solution)/shard_map/norms/all_to_all | solution.py:178
  197.2 6.3 %all-to-all-done.11 = f32[16,1,512]{2,1,0:T(1,128)S(1)} async-done(((f32[16,1,512]{2,1,0:T(1,128)}), f32[16,1,512]{2,1,0:T(1,128)S(1)}, u32[]{:S(2)}, u32[]{:S(2)}) %all-to-all-start.11) | async-done | bytes 32800 | tf_op jit(solution)/shard_map/norms/all_to_all | solution.py:178
  203.5 1.1 outputs.1
  204.6 17.6 %all_to_all.69.mixed_ref = bf16[4,272,512]{2,1,0:T(8,128)(2,1)S(1)} all-to-all(bf16[4,272,512]{2,1,0:T(8,128)(2,1)S(1)} %outputs.1), channel_id=1, replica_groups=mesh['dp'=4,'far'=4,'near'=4,'core'=2,'tensor'=4] {'dp'}, dimensions={0} | all-to-all | bytes 2228224 | tf_op jit(solution)/shard_map/outputs/all_to_all | solution.py:178
  222.2 1.3 merge.1
  (29 shorter events, 2.2 us)
Async XLA Ops:
  0.6 0.8 copy-start
  0.6 16.8 %copy-start.3 = (bf16[1,128,2048]{2,1,0:T(8,128)(2,1)S(1)}, bf16[1,128,2048]{2,1,0:T(8,128)(2,1)}, u32[]{:S(2)}) copy-start(bf16[1,128,2048]{2,1,0:T(8,128)(2,1)} %param.4) | copy-start | bytes 1572868
  2.2 33.6 %all-to-all-start = ((bf16[16,16,512]{2,1,0:T(8,128)(2,1)}), bf16[16,16,512]{2,1,0:T(8,128)(2,1)S(1)}, u32[]{:S(2)}, u32[]{:S(2)}) async-start(bf16[16,16,512]{2,1,0:T(8,128)(2,1)} %broadcast_in_dim.22), calls=%async_computation | async-start | bytes 524288 | tf_op jit(solution)/shard_map/basis/all_to_all | solution.py:178
  17.5 9.9 %collective-permute-start = (bf16[128,512]{1,0:T(8,128)(2,1)S(1)}, bf16[128,512]{1,0:T(8,128)(2,1)S(1)}, u32[]{:S(2)}, u32[]{:S(2)}) collective-permute-start(bf16[128,512]{1,0:T(8,128)(2,1)S(1)} %get-tuple-element.43), channel_id=1, source_target_pairs={{0,128},{128,256},{256,384},{384,0},{1,129},{129,257},{257,385},{3... | collective-permute-start | bytes 393224 | tf_op jit(solution)/shard_map/total/ppermute | solution.py:210
  20.9 6.9 %collective-permute-start.2 = (bf16[128,512]{1,0:T(8,128)(2,1)S(1)}, bf16[128,512]{1,0:T(8,128)(2,1)S(1)}, u32[]{:S(2)}, u32[]{:S(2)}) collective-permute-start(bf16[128,512]{1,0:T(8,128)(2,1)S(1)} %get-tuple-element.44), channel_id=1, source_target_pairs={{0,384},{128,0},{256,128},{384,256},{1,385},{129,1},{257,129},{385... | collective-permute-start | bytes 393224 | tf_op jit(solution)/shard_map/total/ppermute | solution.py:210
  23.4 8.4 %collective-permute-start.1 = (bf16[128,512]{1,0:T(8,128)(2,1)S(1)}, bf16[128,512]{1,0:T(8,128)(2,1)S(1)}, u32[]{:S(2)}, u32[]{:S(2)}) collective-permute-start(bf16[128,512]{1,0:T(8,128)(2,1)S(1)} %get-tuple-element.45), channel_id=1, source_target_pairs={{0,256},{128,384},{256,0},{384,128},{1,257},{129,385},{257,1},{385... | collective-permute-start | bytes 393224 | tf_op jit(solution)/shard_map/total/ppermute | solution.py:210
  52.0 20.6 %all-to-all-start.3 = ((f32[16,32,512]{2,1,0:T(8,128)}), f32[16,32,512]{2,1,0:T(8,128)S(1)}, u32[]{:S(2)}, u32[]{:S(2)}) async-start(f32[16,32,512]{2,1,0:T(8,128)} %broadcast_in_dim.24), calls=%async_computation.3 | async-start | bytes 2097152 | tf_op jit(solution)/shard_map/left/all_to_all | solution.py:178
  79.9 20.9 %all-to-all-start.5 = ((f32[4,296,128]{2,1,0:T(8,128)}), f32[4,296,128]{2,1,0:T(8,128)S(1)}, u32[]{:S(2)}, u32[]{:S(2)}) async-start(f32[4,296,128]{2,1,0:T(8,128)} %pad_maximum_fusion), calls=%async_computation.5 | async-start | bytes 1212416 | tf_op jit(solution)/shard_map/products/all_to_all | solution.py:178
  84.2 9.9 %collective-permute-start.4 = (f32[128,512]{1,0:T(8,128)S(1)}, f32[128,512]{1,0:T(8,128)S(1)}, u32[]{:S(2)}, u32[]{:S(2)}) collective-permute-start(f32[128,512]{1,0:T(8,128)S(1)} %fusion.2.total_ref.refs_0_), channel_id=1, source_target_pairs={{0,384},{128,0},{256,128},{384,256},{1,385},{129,1},{257,129},{385... | collective-permute-start | bytes 786440 | tf_op jit(solution)/shard_map/totals/ppermute | solution.py:219
  88.1 9.7 %collective-permute-start.3 = (f32[128,512]{1,0:T(8,128)S(1)}, f32[128,512]{1,0:T(8,128)S(1)}, u32[]{:S(2)}, u32[]{:S(2)}) collective-permute-start(f32[128,512]{1,0:T(8,128)S(1)} %fusion.2.total_ref.refs_0_), channel_id=1, source_target_pairs={{0,128},{128,256},{256,384},{384,0},{1,129},{129,257},{257,385},{3... | collective-permute-start | bytes 786440 | tf_op jit(solution)/shard_map/totals/ppermute | solution.py:219
  101.5 24.1 %all-to-all-start.6 = ((f32[4,104,128]{2,1,0:T(8,128)}), f32[4,104,128]{2,1,0:T(8,128)S(1)}, u32[]{:S(2)}, u32[]{:S(2)}) async-start(f32[4,104,128]{2,1,0:T(8,128)} %pad_maximum_fusion.1), calls=%async_computation.6 | async-start | bytes 425984 | tf_op jit(solution)/shard_map/products/all_to_all | solution.py:178
  109.8 10.6 %collective-permute-start.5 = (f32[128,512]{1,0:T(8,128)S(1)}, f32[128,512]{1,0:T(8,128)S(1)}, u32[]{:S(2)}, u32[]{:S(2)}) collective-permute-start(f32[128,512]{1,0:T(8,128)S(1)} %fusion.2.total_ref.refs_0_), channel_id=1, source_target_pairs={{0,256},{128,384},{256,0},{384,128},{1,257},{129,385},{257,1},{385... | collective-permute-start | bytes 786440 | tf_op jit(solution)/shard_map/totals/ppermute | solution.py:219
  126.6 16.5 %all-to-all-start.7 = ((f32[32,40,128]{2,1,0:T(8,128)}), f32[32,40,128]{2,1,0:T(8,128)S(1)}, u32[]{:S(2)}, u32[]{:S(2)}) async-start(f32[32,40,128]{2,1,0:T(8,128)} %broadcast_in_dim.27), calls=%async_computation.7 | async-start | bytes 1310720 | tf_op jit(solution)/shard_map/products/all_to_all | solution.py:178
  143.7 20.4 %all-to-all-start.8 = ((f32[4,64,128]{2,1,0:T(8,128)}), f32[4,64,128]{2,1,0:T(8,128)S(1)}, u32[]{:S(2)}, u32[]{:S(2)}) async-start(f32[4,64,128]{2,1,0:T(8,128)} %broadcast_in_dim.28), calls=%async_computation.8 | async-start | bytes 262144 | tf_op jit(solution)/shard_map/factor/all_to_all | solution.py:178
  165.0 18.3 %all-to-all-start.9 = ((f32[4,4,64,128]{3,2,1,0:T(8,128)}), f32[4,4,64,128]{3,2,1,0:T(8,128)}, u32[]{:S(2)}, u32[]{:S(2)}) async-start(f32[4,4,64,128]{3,2,1,0:T(8,128)} %broadcast_in_dim.29), calls=%async_computation.9 | async-start | bytes 1048576 | tf_op jit(solution)/shard_map/factor/all_to_all | solution.py:178
  179.8 0.8 copy-start.1
  184.4 4.7 %copy-start.2 = (f32[256,512]{1,0:T(8,128)S(1)}, f32[256,512]{1,0:T(8,128)}, u32[]{:S(2)}) copy-start(f32[256,512]{1,0:T(8,128)} %copy-done.1) | copy-start | bytes 1572868
  192.2 11.3 %all-to-all-start.11 = ((f32[16,1,512]{2,1,0:T(1,128)}), f32[16,1,512]{2,1,0:T(1,128)S(1)}, u32[]{:S(2)}, u32[]{:S(2)}) async-start(f32[16,1,512]{2,1,0:T(1,128)} %broadcast_in_dim.32), calls=%async_computation.11 | async-start | bytes 65536 | tf_op jit(solution)/shard_map/norms/all_to_all | solution.py:178

commit v3 on v2

--- a/solution.py
+++ b/solution.py
@@ -11,6 +11,7 @@
 
 HIGH = lax.Precision.HIGHEST
 EDGE = 128
+BOTH = ("dp", "tensor")
 VMEM = pl.BlockSpec(memory_space=pltpu.VMEM)
 SMEM = pl.BlockSpec(memory_space=pltpu.SMEM)
 
@@ -26,7 +27,9 @@
         out_shape=[jax.ShapeDtypeStruct(s, t) for s, t in zip(shapes, dtypes)],
         in_specs=[SMEM] * scalars + [VMEM] * (len(args) - scalars),
         out_specs=[VMEM] * len(shapes),
-        scratch_shapes=[pltpu.VMEM(shape, jnp.float32) for shape in scratch],
+        scratch_shapes=[
+            pltpu.VMEM(*s) if isinstance(s[-1], type) else pltpu.VMEM(s, jnp.float32) for s in scratch
+        ],
         compiler_params=pltpu.CompilerParams(vmem_limit_bytes=32 * 1024 * 1024),
         cost_estimate=pl.CostEstimate(flops=flops, bytes_accessed=4 * 1024 * 1024, transcendentals=0),
         name=kernel.func.__name__ if isinstance(kernel, functools.partial) else kernel.__name__,
@@ -90,12 +93,16 @@
     return [(k, j) for k in range(count) for j in range(k, count)]
 
 
-def factor_top(gram_ref, top_ref, rest_ref, work):
+def factor_top(core_ref, own_ref, other_ref, top_ref, rest_ref, work, gram):
     size = work.shape[0]
     count = size // EDGE
+    slot = own_ref.shape[1]
+    for refs, core in ((own_ref, core_ref[0]), (other_ref, 1 - core_ref[0])):
+        for j in range(refs.shape[0]):
+            gram[pl.ds(pl.multiple_of((2 * j + core) * slot, 8), slot), :] = refs[j]
     work[...] = jnp.zeros_like(work)
     for at, (k, j) in enumerate(upper_blocks(count)):
-        work[k * EDGE : (k + 1) * EDGE, j * EDGE : (j + 1) * EDGE] = gram_ref[at * EDGE : (at + 1) * EDGE, :]
+        work[k * EDGE : (k + 1) * EDGE, j * EDGE : (j + 1) * EDGE] = gram[at * EDGE : (at + 1) * EDGE, :]
     eliminate(work, top_ref, 0, count // 2, 0)
     rest_ref[...] = work[size // 2 :, :]
 
@@ -110,7 +117,21 @@
     basis_ref[:, half:] = dot(left_ref[...], low_ref[...], ((1,), (1,)))
 
 
-def products(near, far, place_ref, left_ref, total_ref, out_ref, gram):
+def left_part(core_ref, own_ref, other_ref, total_ref, out_ref, basis):
+    count, ranks, _ = own_ref.shape
+    for refs, core in ((own_ref, core_ref[0]), (other_ref, 1 - core_ref[0])):
+        for z in range(count):
+            basis[pl.ds(pl.multiple_of((2 * z + core) * ranks, ranks), ranks), :] = refs[z]
+    rest = total_ref[...]
+    left = jnp.zeros(out_ref.shape, jnp.float32)
+    for _ in range(3):
+        part = rest.astype(jnp.bfloat16)
+        left += lax.dot_general(part, basis[...], (((1,), (1,)), ((), ())), preferred_element_type=jnp.float32)
+        rest -= part.astype(jnp.float32)
+    out_ref[...] = left
+
+
+def products(near, far, place_ref, core_ref, left_ref, total_ref, keep_ref, send_ref, out, gram):
     left = left_ref[...]
     rank = left.shape[1]
     cols = total_ref.shape[1]
@@ -121,7 +142,7 @@
         to, rest = divmod(i, near * far)
         for j in range(blocks):
             at = (rest * blocks + j) * piece
-            out_ref[to, at : at + piece, :] = prod[i * piece : (i + 1) * piece, j * EDGE : (j + 1) * EDGE]
+            out[to, at : at + piece, :] = prod[i * piece : (i + 1) * piece, j * EDGE : (j + 1) * EDGE]
     at = 0
     for k in range(rank // EDGE):
         row = dot(left[:, k * EDGE : (k + 1) * EDGE], left[:, k * EDGE :], ((0,), (0,)))
@@ -129,15 +150,19 @@
             gram[at : at + EDGE, :] = row[:, j * EDGE : (j + 1) * EDGE]
             at += EDGE
     begin = near * far * blocks * piece
-    slot = out_ref.shape[1] - begin
+    slot = out.shape[1] - begin
     for to in range(2):
-        out_ref[to, begin:, :] = gram[pl.ds(pl.multiple_of((2 * place_ref[0] + to) * slot, 8), slot), :]
-
-
-def finish(prod_ref, top_ref, low_ref, right_ref, squares_ref, prod):
+        out[to, begin:, :] = gram[pl.ds(pl.multiple_of((2 * place_ref[0] + to) * slot, 8), slot), :]
+    keep_ref[...] = out[core_ref[0]]
+    send_ref[...] = out[1 - core_ref[0]]
+
+
+def finish(core_ref, own_ref, other_ref, top_ref, low_ref, right_ref, squares_ref, prod):
     half = top_ref.shape[0]
-    for j in range(prod_ref.shape[1]):
-        prod[:, j * EDGE : (j + 1) * EDGE] = prod_ref[:, j].reshape(2 * half, EDGE)
+    for refs, core in ((own_ref, core_ref[0]), (other_ref, 1 - core_ref[0])):
+        at = pl.ds(pl.multiple_of(core * half, half), half)
+        for j in range(refs.shape[1]):
+            prod[at, j * EDGE : (j + 1) * EDGE] = refs[:, j].reshape(half, EDGE)
     top = dot(top_ref[:, :half], prod[:half, :], ((1,), (0,)))
     low = dot(low_ref[...], prod[...], ((1,), (0,)))
     right_ref[:half, :] = top
@@ -182,6 +207,10 @@
     return swap(jnp.broadcast_to(x[None], (lax.axis_size(axis),) + x.shape), axis)
 
 
+def other_core(x):
+    return lax.ppermute(x, "core", [(0, 1), (1, 0)])
+
+
 def per_device(momentum, grads, right_basis):
     rows, local_cols = momentum.shape
     n_dp, n_far, n_near, n_tensor = (lax.axis_size(a) for a in ("dp", "far", "near", "tensor"))
@@ -193,7 +222,8 @@
     factor_scale = math.sqrt(rows * n_fsdp * local_cols * n_tensor / rank)
     d = lax.axis_index("dp")
     me = lax.axis_index(("far", "near", "core")).reshape(1)
-    place = lax.axis_index(("dp", "tensor")).reshape(1)
+    place = lax.axis_index(BOTH).reshape(1)
+    core = lax.axis_index("core").reshape(1)
     slot = len(upper_blocks(rank // EDGE)) * EDGE // n_slots
 
     def turn(k):
@@ -202,7 +232,7 @@
     with jax.named_scope("basis"):
         mine = lax.dynamic_slice_in_dim(right_basis.T, d * cols, cols, 1)
         part = share(mine, ("far", "near"))
-        basis_t = share(part, "core").transpose(1, 0, 2, 3).reshape(rank, cols)
+        other = other_core(part)
     with jax.named_scope("total"):
         def column(x, k):
             return lax.dynamic_slice_in_dim(x, (d + k) % n_dp * cols, cols, 1)
@@ -211,23 +241,22 @@
         total = sum((b.astype(jnp.float32) for b in blocks), column(grads[0], 0).astype(jnp.float32))
         total = column(momentum, 0) + total
     with jax.named_scope("left"):
-        partial = dot(total, basis_t.astype(jnp.float32), ((1,), (1,)))
-        partial = jnp.sum(swap(partial.reshape(n_dp, rows // n_dp, rank), "dp"), axis=0)
-        partial = share(partial, ("dp", "tensor")).reshape(n_dp, n_tensor, rows // n_dp, rank)
-        left = jnp.sum(partial, axis=1).reshape(rows, rank)
+        partial = call(left_part, [(rows, rank)], (core, part, other, total), 10**9, [((rank, cols), jnp.bfloat16)], 1)[0]
+        partial = swap(partial.reshape(n_dp * n_tensor, rows // (n_dp * n_tensor), rank), BOTH)
+        left = share(jnp.sum(partial, axis=0), BOTH).reshape(rows, rank)
     with jax.named_scope("totals"):
         totals = [total] + [lax.ppermute(total, "dp", turn(k)) for k in range(1, n_dp)]
     with jax.named_scope("products"):
         prod_rows = rank * cols // EDGE // 2
-        both = call(
+        keep, send = call(
             functools.partial(products, n_near, n_far),
-            [(2, prod_rows + slot, EDGE)],
-            (place, left, total),
+            [(prod_rows + slot, EDGE)] * 2,
+            (place, core, left, total),
             10**9,
-            [(n_slots * slot, EDGE)],
-            1,
-        )[0]
-        both = jnp.sum(swap(both, "core"), axis=0)
+            [(2, prod_rows + slot, EDGE), (n_slots * slot, EDGE)],
+            2,
+        )
+        both = keep + other_core(send)
         for axis, n in (("near", n_near), ("far", n_far)):
             prod_rows = both.shape[0] - slot
             prod = both[:prod_rows].reshape(n, prod_rows // n, EDGE)
@@ -239,23 +268,35 @@
                 both, totals[2] = lax.optimization_barrier((both, totals[2]))
             both = jnp.sum(both, axis=0)
         prod, gram = both[:-slot], both[-slot:]
-        gram = share(gram, ("dp", "tensor", "core")).reshape(n_slots * slot, EDGE)
+        gram = share(gram, BOTH)
         prod, gram = lax.optimization_barrier((prod, gram))
     with jax.named_scope("factor"):
         half = (rank // 2, rank)
-        top, rest = call(factor_top, [half, half], (gram,), 10**10, [(rank, rank)])
+        top, rest = call(
+            factor_top,
+            [half, half],
+            (core, gram, other_core(gram)),
+            10**10,
+            [(rank, rank), (n_slots * slot, EDGE)],
+            1,
+        )
         prod = share(prod, "far")
         prod, rest = lax.optimization_barrier((prod, rest))
         low, left_basis = call(factor_rest, [half, (rows, rank)], (rest, top, left), 10**10, [half])
         prod = share(prod, "near")
         prod, low = lax.optimization_barrier((prod, low))
     with jax.named_scope("right"):
-        prod = share(prod, "core").reshape(n_fsdp, cols // EDGE, rank_local, EDGE)
+        prod = prod.reshape(n_fsdp // 2, cols // EDGE, rank_local, EDGE)
         right_t, squares = call(
-            finish, [(rank, cols), (8, rank)], (prod, top, low), 2 * 10**9, [(rank, cols)]
+            finish,
+            [(rank, cols), (8, rank)],
+            (core, prod, other_core(prod), top, low),
+            2 * 10**9,
+            [(rank, cols)],
+            1,
         )
     with jax.named_scope("norms"):
-        squares = share(squares[:1], ("dp", "tensor")).reshape(n_dp * n_tensor, rank)
+        squares = share(squares[:1], BOTH).reshape(n_dp * n_tensor, rank)
     with jax.named_scope("outputs"):
         mixed = call(
             functools.partial(outputs, factor_scale),

time: 225 us -> 212 us (0.942)
  the two profiles are of different devices: /device:TPU:2 before, /device:TPU:32 now
where the time goes in v3:
time: 212 us; the launch traced here: 210 us
  starting transfers between devices  70.5 us (33%)
  waiting for transfers between devices  66.4 us (31%)
  blocking collectives  33 us (16%)
  Pallas kernels  28.5 us (13%)
  local copies, waits for them, and re-layouts  8.21 us (4%)
  other arithmetic  2.72 us (1%)
    all_to_all x8, waiting for transfers between devices, swap(): return lax.all_to_all(x, axis, 0, 0, tiled=True)  47.4 us
    all_to_all x8, starting transfers between devices, swap(): return lax.all_to_all(x, axis, 0, 0, tiled=True)  43.3 us
    all_to_all x2, blocking collectives, swap(): return lax.all_to_all(x, axis, 0, 0, tiled=True)  33 us
    pallas_call x7, Pallas kernels, call(): pl.pallas_call(kernel, out_shape=[jax.ShapeDtypeStruct(s, t) for s, t in...  28.5 us
    ppermute x3, waiting for transfers between devices, per_device(): lax.ppermute(total, 'dp', turn(k))  14.8 us
    ppermute x3, starting transfers between devices, per_device(): lax.ppermute(column(grads[0], k), 'dp', turn(k))  10.8 us
    ppermute x3, starting transfers between devices, per_device(): lax.ppermute(total, 'dp', turn(k))  8.74 us
    ppermute x4, starting transfers between devices, other_core(): return lax.ppermute(x, 'core', [(0, 1), (1, 0)])  7.65 us
  transfers between devices with their start and end apart: 18, of which 12 were waited for; matrix products, arithmetic and copies ran while one was open for 1% of the time, Pallas kernels for 10%

profile of v3, /device:TPU:32, one launch (start us, length us, event | category | flops | bytes accessed | tf_op | source)
XLA Modules:
  0.0 210.4 jit_solution(6787734997540447486)
XLA Ops:
  0.7 0.8 copy-done
  1.5 0.7 broadcast_in_dim.18
  2.2 15.2 %all-to-all-start = ((bf16[16,16,512]{2,1,0:T(8,128)(2,1)}), bf16[16,16,512]{2,1,0:T(8,128)(2,1)S(1)}, u32[]{:S(2)}, u32[]{:S(2)}) async-start(bf16[16,16,512]{2,1,0:T(8,128)(2,1)} %broadcast_in_dim.18), calls=%async_computation | async-start | bytes 524288 | tf_op jit(solution)/shard_map/basis/all_to_all | solution.py:203
  17.5 3.4 %collective-permute-start.1 = (bf16[128,512]{1,0:T(8,128)(2,1)S(1)}, bf16[128,512]{1,0:T(8,128)(2,1)S(1)}, u32[]{:S(2)}, u32[]{:S(2)}) collective-permute-start(bf16[128,512]{1,0:T(8,128)(2,1)S(1)} %get-tuple-element.47), channel_id=1, source_target_pairs={{0,128},{128,256},{256,384},{384,0},{1,129},{129,257},{257,385},{3... | collective-permute-start | bytes 393224 | tf_op jit(solution)/shard_map/total/ppermute | solution.py:240
  20.9 3.7 %collective-permute-start.3 = (bf16[128,512]{1,0:T(8,128)(2,1)S(1)}, bf16[128,512]{1,0:T(8,128)(2,1)S(1)}, u32[]{:S(2)}, u32[]{:S(2)}) collective-permute-start(bf16[128,512]{1,0:T(8,128)(2,1)S(1)} %get-tuple-element.48), channel_id=1, source_target_pairs={{0,384},{128,0},{256,128},{384,256},{1,385},{129,1},{257,129},{385... | collective-permute-start | bytes 393224 | tf_op jit(solution)/shard_map/total/ppermute | solution.py:240
  24.5 3.7 %collective-permute-start.2 = (bf16[128,512]{1,0:T(8,128)(2,1)S(1)}, bf16[128,512]{1,0:T(8,128)(2,1)S(1)}, u32[]{:S(2)}, u32[]{:S(2)}) collective-permute-start(bf16[128,512]{1,0:T(8,128)(2,1)S(1)} %get-tuple-element.49), channel_id=1, source_target_pairs={{0,256},{128,384},{256,0},{384,128},{1,257},{129,385},{257,1},{385... | collective-permute-start | bytes 393224 | tf_op jit(solution)/shard_map/total/ppermute | solution.py:240
  28.3 7.1 %all-to-all-done.own_ref = bf16[16,16,512]{2,1,0:T(8,128)(2,1)S(1)} async-done(((bf16[16,16,512]{2,1,0:T(8,128)(2,1)}), bf16[16,16,512]{2,1,0:T(8,128)(2,1)S(1)}, u32[]{:S(2)}, u32[]{:S(2)}) %all-to-all-start) | async-done | bytes 262176 | tf_op jit(solution)/shard_map/basis/all_to_all | solution.py:203
  35.3 1.9 collective-permute-start
  37.3 1.0 fusion.2.total_ref.refs_0_
  39.4 15.6 %all_to_all.50 = f32[16,8,512]{2,1,0:T(8,128)S(1)} all-to-all(f32[16,8,512]{2,1,0:T(8,128)S(1)} %bitcast.29), channel_id=1, replica_groups=mesh['dp'=4,'far'=4,'near'=4,'core'=2,'tensor'=4] {'dp','tensor'}, dimensions={0} | all-to-all | bytes 524288 | tf_op jit(solution)/shard_map/left/all_to_all | solution.py:203
  55.1 0.7 broadcast_in_dim.19
  55.8 3.6 %all-to-all-start.2 = ((f32[16,8,512]{2,1,0:T(8,128)}), f32[16,8,512]{2,1,0:T(8,128)S(1)}, u32[]{:S(2)}, u32[]{:S(2)}) async-start(f32[16,8,512]{2,1,0:T(8,128)} %broadcast_in_dim.19), calls=%async_computation.2 | async-start | bytes 524288 | tf_op jit(solution)/shard_map/left/all_to_all | solution.py:203
  59.5 8.5 %all-to-all-done.2 = f32[16,8,512]{2,1,0:T(8,128)S(1)} async-done(((f32[16,8,512]{2,1,0:T(8,128)}), f32[16,8,512]{2,1,0:T(8,128)S(1)}, u32[]{:S(2)}, u32[]{:S(2)}) %all-to-all-start.2) | async-done | bytes 262176 | tf_op jit(solution)/shard_map/left/all_to_all | solution.py:203
  67.9 1.6 products.1
  69.5 1.9 collective-permute-start.4
  71.5 1.9 collective-permute-done.4
  73.5 0.9 pad_maximum_fusion
  74.4 4.9 %all-to-all-start.3 = ((f32[4,296,128]{2,1,0:T(8,128)}), f32[4,296,128]{2,1,0:T(8,128)S(1)}, u32[]{:S(2)}, u32[]{:S(2)}) async-start(f32[4,296,128]{2,1,0:T(8,128)} %pad_maximum_fusion), calls=%async_computation.3 | async-start | bytes 1212416 | tf_op jit(solution)/shard_map/products/all_to_all | solution.py:203
  79.3 3.0 %collective-permute-start.6 = (f32[128,512]{1,0:T(8,128)S(1)}, f32[128,512]{1,0:T(8,128)S(1)}, u32[]{:S(2)}, u32[]{:S(2)}) collective-permute-start(f32[128,512]{1,0:T(8,128)S(1)} %fusion.2.total_ref.refs_0_), channel_id=1, source_target_pairs={{0,384},{128,0},{256,128},{384,256},{1,385},{129,1},{257,129},{385... | collective-permute-start | bytes 786440 | tf_op jit(solution)/shard_map/totals/ppermute | solution.py:248
  82.3 2.9 %collective-permute-start.5 = (f32[128,512]{1,0:T(8,128)S(1)}, f32[128,512]{1,0:T(8,128)S(1)}, u32[]{:S(2)}, u32[]{:S(2)}) collective-permute-start(f32[128,512]{1,0:T(8,128)S(1)} %fusion.2.total_ref.refs_0_), channel_id=1, source_target_pairs={{0,128},{128,256},{256,384},{384,0},{1,129},{129,257},{257,385},{3... | collective-permute-start | bytes 786440 | tf_op jit(solution)/shard_map/totals/ppermute | solution.py:248
  85.1 3.8 %collective-permute-done.6.refs_3_ = f32[128,512]{1,0:T(8,128)S(1)} collective-permute-done((f32[128,512]{1,0:T(8,128)S(1)}, f32[128,512]{1,0:T(8,128)S(1)}, u32[]{:S(2)}, u32[]{:S(2)}) %collective-permute-start.6) | collective-permute-done | bytes 262176 | tf_op jit(solution)/shard_map/totals/ppermute | solution.py:248
  89.0 3.9 %collective-permute-done.5.refs_1_ = f32[128,512]{1,0:T(8,128)S(1)} collective-permute-done((f32[128,512]{1,0:T(8,128)S(1)}, f32[128,512]{1,0:T(8,128)S(1)}, u32[]{:S(2)}, u32[]{:S(2)}) %collective-permute-start.5) | collective-permute-done | bytes 262176 | tf_op jit(solution)/shard_map/totals/ppermute | solution.py:248
  93.0 0.7 pad_maximum_fusion.1
  93.7 5.4 %all-to-all-start.4 = ((f32[4,104,128]{2,1,0:T(8,128)}), f32[4,104,128]{2,1,0:T(8,128)S(1)}, u32[]{:S(2)}, u32[]{:S(2)}) async-start(f32[4,104,128]{2,1,0:T(8,128)} %pad_maximum_fusion.1), calls=%async_computation.4 | async-start | bytes 425984 | tf_op jit(solution)/shard_map/products/all_to_all | solution.py:203
  99.0 2.9 %collective-permute-start.7 = (f32[128,512]{1,0:T(8,128)S(1)}, f32[128,512]{1,0:T(8,128)S(1)}, u32[]{:S(2)}, u32[]{:S(2)}) collective-permute-start(f32[128,512]{1,0:T(8,128)S(1)} %fusion.2.total_ref.refs_0_), channel_id=1, source_target_pairs={{0,256},{128,384},{256,0},{384,128},{1,257},{129,385},{257,1},{385... | collective-permute-start | bytes 786440 | tf_op jit(solution)/shard_map/totals/ppermute | solution.py:248
  102.0 7.1 %collective-permute-done.7.refs_2_ = f32[128,512]{1,0:T(8,128)S(1)} collective-permute-done((f32[128,512]{1,0:T(8,128)S(1)}, f32[128,512]{1,0:T(8,128)S(1)}, u32[]{:S(2)}, u32[]{:S(2)}) %collective-permute-start.7) | collective-permute-done | bytes 262176 | tf_op jit(solution)/shard_map/totals/ppermute | solution.py:248
  109.0 9.3 %all-to-all-done.4 = f32[4,104,128]{2,1,0:T(8,128)S(1)} async-done(((f32[4,104,128]{2,1,0:T(8,128)}), f32[4,104,128]{2,1,0:T(8,128)S(1)}, u32[]{:S(2)}, u32[]{:S(2)}) %all-to-all-start.4) | async-done | bytes 213024 | tf_op jit(solution)/shard_map/products/all_to_all | solution.py:203
  118.4 0.7 broadcast_in_dim.22
  119.1 3.5 %all-to-all-start.5 = ((f32[16,40,128]{2,1,0:T(8,128)}), f32[16,40,128]{2,1,0:T(8,128)S(1)}, u32[]{:S(2)}, u32[]{:S(2)}) async-start(f32[16,40,128]{2,1,0:T(8,128)} %broadcast_in_dim.22), calls=%async_computation.5 | async-start | bytes 655360 | tf_op jit(solution)/shard_map/products/all_to_all | solution.py:203
  122.7 8.8 %all-to-all-done.5.own_ref = f32[16,40,128]{2,1,0:T(8,128)S(1)} async-done(((f32[16,40,128]{2,1,0:T(8,128)}), f32[16,40,128]{2,1,0:T(8,128)S(1)}, u32[]{:S(2)}, u32[]{:S(2)}) %all-to-all-start.5) | async-done | bytes 327712 | tf_op jit(solution)/shard_map/products/all_to_all | solution.py:203
  131.4 1.9 collective-permute-start.8
  134.0 3.3 %all-to-all-start.6 = ((f32[4,64,128]{2,1,0:T(8,128)}), f32[4,64,128]{2,1,0:T(8,128)S(1)}, u32[]{:S(2)}, u32[]{:S(2)}) async-start(f32[4,64,128]{2,1,0:T(8,128)} %broadcast_in_dim.23), calls=%async_computation.6 | async-start | bytes 262144 | tf_op jit(solution)/shard_map/factor/all_to_all | solution.py:203
  137.4 10.8 %factor_top.1 = (f32[256,512]{1,0:T(8,128)S(1)}, f32[256,512]{1,0:T(8,128)S(1)}) custom-call(s32[1]{0:T(128)} %bitcast.2.core_ref, f32[16,40,128]{2,1,0:T(8,128)S(1)} %all-to-all-done.5.own_ref, f32[16,40,128]{2,1,0:T(8,128)S(1)} %collective-permute-done.8.other_ref), custom_call_target="tpu_custom_call" | custom-call | flops 10000000000 | bytes 4194304 | tf_op jit(solution)/shard_map/factor/factor_top/pallas_call | solution.py:25
  148.2 6.2 %all-to-all-done.6 = f32[4,64,128]{2,1,0:T(8,128)S(1)} async-done(((f32[4,64,128]{2,1,0:T(8,128)}), f32[4,64,128]{2,1,0:T(8,128)S(1)}, u32[]{:S(2)}, u32[]{:S(2)}) %all-to-all-start.6) | async-done | bytes 131104 | tf_op jit(solution)/shard_map/factor/all_to_all | solution.py:203
  154.3 0.8 broadcast_in_dim.24
  155.2 3.6 %all-to-all-start.7 = ((f32[4,4,64,128]{3,2,1,0:T(8,128)}), f32[4,4,64,128]{3,2,1,0:T(8,128)S(1)}, u32[]{:S(2)}, u32[]{:S(2)}) async-start(f32[4,4,64,128]{3,2,1,0:T(8,128)} %broadcast_in_dim.24), calls=%async_computation.7 | async-start | bytes 1048576 | tf_op jit(solution)/shard_map/factor/all_to_all | solution.py:203
  158.9 1.0 copy-done.4
  159.9 10.5 %factor_rest.1 = (f32[256,512]{1,0:T(8,128)S(1)}, f32[128,512]{1,0:T(8,128)S(1)}) custom-call(f32[256,512]{1,0:T(8,128)S(1)} %copy-done.4, f32[256,512]{1,0:T(8,128)S(1)} %get-tuple-element.34.top_ref, f32[128,512]{1,0:T(8,128)S(1)} %bitcast.28), custom_call_target="tpu_custom_call" | custom-call | flops 10000000000 | bytes 4194304 | tf_op jit(solution)/shard_map/factor/factor_rest/pallas_call | solution.py:25
  170.4 0.8 copy-done.1
  171.2 1.9 collective-permute-start.9
  173.1 1.9 collective-permute-done.9.other_ref
  175.0 1.0 copy-done.2
  176.0 2.5 %finish.1 = (f32[512,512]{1,0:T(8,128)S(1)}, f32[8,512]{1,0:T(8,128)S(1)}) custom-call(s32[1]{0:T(128)} %bitcast.2.core_ref, f32[16,4,16,128]{3,2,1,0:T(8,128)S(1)} %bitcast.26, f32[16,4,16,128]{3,2,1,0:T(8,128)S(1)} %collective-permute-done.9.other_ref, f32[256,512]{1,0:T(8,128)S(1)} %get-tuple-element.34.top_ref, f32[256,512]{1,0:T(8,128)S(1)} %copy-done.2), custom_call_target="tpu_custom_call" | custom-call | flops 2000000000 | bytes 4194304 | tf_op jit(solution)/shard_map/right/finish/pallas_call | solution.py:25
  179.2 3.7 %all-to-all-start.8 = ((f32[16,1,512]{2,1,0:T(1,128)}), f32[16,1,512]{2,1,0:T(1,128)S(1)}, u32[]{:S(2)}, u32[]{:S(2)}) async-start(f32[16,1,512]{2,1,0:T(1,128)} %broadcast_in_dim.26), calls=%async_computation.8 | async-start | bytes 65536 | tf_op jit(solution)/shard_map/norms/all_to_all | solution.py:203
  182.9 7.6 %all-to-all-done.8 = f32[16,1,512]{2,1,0:T(1,128)S(1)} async-done(((f32[16,1,512]{2,1,0:T(1,128)}), f32[16,1,512]{2,1,0:T(1,128)S(1)}, u32[]{:S(2)}, u32[]{:S(2)}) %all-to-all-start.8) | async-done | bytes 32800 | tf_op jit(solution)/shard_map/norms/all_to_all | solution.py:203
  190.6 1.1 outputs.1
  191.7 17.4 %all_to_all.51.mixed_ref = bf16[4,272,512]{2,1,0:T(8,128)(2,1)S(1)} all-to-all(bf16[4,272,512]{2,1,0:T(8,128)(2,1)S(1)} %outputs.1), channel_id=1, replica_groups=mesh['dp'=4,'far'=4,'near'=4,'core'=2,'tensor'=4] {'dp'}, dimensions={0} | all-to-all | bytes 2228224 | tf_op jit(solution)/shard_map/outputs/all_to_all | solution.py:203
  209.1 1.3 merge.1
  (34 shorter events, 2.7 us)
Async XLA Ops:
  0.6 0.8 copy-start
  0.6 16.8 %copy-start.5 = (bf16[1,128,2048]{2,1,0:T(8,128)(2,1)S(1)}, bf16[1,128,2048]{2,1,0:T(8,128)(2,1)}, u32[]{:S(2)}) copy-start(bf16[1,128,2048]{2,1,0:T(8,128)(2,1)} %param.4) | copy-start | bytes 1572868
  2.2 33.1 %all-to-all-start = ((bf16[16,16,512]{2,1,0:T(8,128)(2,1)}), bf16[16,16,512]{2,1,0:T(8,128)(2,1)S(1)}, u32[]{:S(2)}, u32[]{:S(2)}) async-start(bf16[16,16,512]{2,1,0:T(8,128)(2,1)} %broadcast_in_dim.18), calls=%async_computation | async-start | bytes 524288 | tf_op jit(solution)/shard_map/basis/all_to_all | solution.py:203
  17.5 19.8 %collective-permute-start.1 = (bf16[128,512]{1,0:T(8,128)(2,1)S(1)}, bf16[128,512]{1,0:T(8,128)(2,1)S(1)}, u32[]{:S(2)}, u32[]{:S(2)}) collective-permute-start(bf16[128,512]{1,0:T(8,128)(2,1)S(1)} %get-tuple-element.47), channel_id=1, source_target_pairs={{0,128},{128,256},{256,384},{384,0},{1,129},{129,257},{257,385},{3... | collective-permute-start | bytes 393224 | tf_op jit(solution)/shard_map/total/ppermute | solution.py:240
  20.9 16.4 %collective-permute-start.3 = (bf16[128,512]{1,0:T(8,128)(2,1)S(1)}, bf16[128,512]{1,0:T(8,128)(2,1)S(1)}, u32[]{:S(2)}, u32[]{:S(2)}) collective-permute-start(bf16[128,512]{1,0:T(8,128)(2,1)S(1)} %get-tuple-element.48), channel_id=1, source_target_pairs={{0,384},{128,0},{256,128},{384,256},{1,385},{129,1},{257,129},{385... | collective-permute-start | bytes 393224 | tf_op jit(solution)/shard_map/total/ppermute | solution.py:240
  24.5 12.7 %collective-permute-start.2 = (bf16[128,512]{1,0:T(8,128)(2,1)S(1)}, bf16[128,512]{1,0:T(8,128)(2,1)S(1)}, u32[]{:S(2)}, u32[]{:S(2)}) collective-permute-start(bf16[128,512]{1,0:T(8,128)(2,1)S(1)} %get-tuple-element.49), channel_id=1, source_target_pairs={{0,256},{128,384},{256,0},{384,128},{1,257},{129,385},{257,1},{385... | collective-permute-start | bytes 393224 | tf_op jit(solution)/shard_map/total/ppermute | solution.py:240
  35.3 3.4 %collective-permute-start = (bf16[16,16,512]{2,1,0:T(8,128)(2,1)S(1)}, bf16[16,16,512]{2,1,0:T(8,128)(2,1)S(1)}, u32[]{:S(2)}, u32[]{:S(2)}) collective-permute-start(bf16[16,16,512]{2,1,0:T(8,128)(2,1)S(1)} %all-to-all-done.own_ref), channel_id=1, source_target_pairs={{0,4},{4,0},{1,5},{5,1},{2,6},{6,2},{3,7},{7,3},{8,12},{12,8},{9,1... | collective-permute-start | bytes 786440 | tf_op jit(solution)/shard_map/basis/ppermute | solution.py:211
  55.8 12.1 %all-to-all-start.2 = ((f32[16,8,512]{2,1,0:T(8,128)}), f32[16,8,512]{2,1,0:T(8,128)S(1)}, u32[]{:S(2)}, u32[]{:S(2)}) async-start(f32[16,8,512]{2,1,0:T(8,128)} %broadcast_in_dim.19), calls=%async_computation.2 | async-start | bytes 524288 | tf_op jit(solution)/shard_map/left/all_to_all | solution.py:203
  69.5 3.8 %collective-permute-start.4 = (f32[1064,128]{1,0:T(8,128)S(1)}, f32[1064,128]{1,0:T(8,128)S(1)}, u32[]{:S(2)}, u32[]{:S(2)}) collective-permute-start(f32[1064,128]{1,0:T(8,128)S(1)} %get-tuple-element.26), channel_id=1, source_target_pairs={{0,4},{4,0},{1,5},{5,1},{2,6},{6,2},{3,7},{7,3},{8,12},{12,8},{9,1... | collective-permute-start | bytes 1634312 | tf_op jit(solution)/shard_map/products/ppermute | solution.py:211
  74.4 18.5 %all-to-all-start.3 = ((f32[4,296,128]{2,1,0:T(8,128)}), f32[4,296,128]{2,1,0:T(8,128)S(1)}, u32[]{:S(2)}, u32[]{:S(2)}) async-start(f32[4,296,128]{2,1,0:T(8,128)} %pad_maximum_fusion), calls=%async_computation.3 | async-start | bytes 1212416 | tf_op jit(solution)/shard_map/products/all_to_all | solution.py:203
  79.3 9.7 %collective-permute-start.6 = (f32[128,512]{1,0:T(8,128)S(1)}, f32[128,512]{1,0:T(8,128)S(1)}, u32[]{:S(2)}, u32[]{:S(2)}) collective-permute-start(f32[128,512]{1,0:T(8,128)S(1)} %fusion.2.total_ref.refs_0_), channel_id=1, source_target_pairs={{0,384},{128,0},{256,128},{384,256},{1,385},{129,1},{257,129},{385... | collective-permute-start | bytes 786440 | tf_op jit(solution)/shard_map/totals/ppermute | solution.py:248
  82.3 10.6 %collective-permute-start.5 = (f32[128,512]{1,0:T(8,128)S(1)}, f32[128,512]{1,0:T(8,128)S(1)}, u32[]{:S(2)}, u32[]{:S(2)}) collective-permute-start(f32[128,512]{1,0:T(8,128)S(1)} %fusion.2.total_ref.refs_0_), channel_id=1, source_target_pairs={{0,128},{128,256},{256,384},{384,0},{1,129},{129,257},{257,385},{3... | collective-permute-start | bytes 786440 | tf_op jit(solution)/shard_map/totals/ppermute | solution.py:248
  93.7 24.7 %all-to-all-start.4 = ((f32[4,104,128]{2,1,0:T(8,128)}), f32[4,104,128]{2,1,0:T(8,128)S(1)}, u32[]{:S(2)}, u32[]{:S(2)}) async-start(f32[4,104,128]{2,1,0:T(8,128)} %pad_maximum_fusion.1), calls=%async_computation.4 | async-start | bytes 425984 | tf_op jit(solution)/shard_map/products/all_to_all | solution.py:203
  99.0 10.0 %collective-permute-start.7 = (f32[128,512]{1,0:T(8,128)S(1)}, f32[128,512]{1,0:T(8,128)S(1)}, u32[]{:S(2)}, u32[]{:S(2)}) collective-permute-start(f32[128,512]{1,0:T(8,128)S(1)} %fusion.2.total_ref.refs_0_), channel_id=1, source_target_pairs={{0,256},{128,384},{256,0},{384,128},{1,257},{129,385},{257,1},{385... | collective-permute-start | bytes 786440 | tf_op jit(solution)/shard_map/totals/ppermute | solution.py:248
  119.1 12.3 %all-to-all-start.5 = ((f32[16,40,128]{2,1,0:T(8,128)}), f32[16,40,128]{2,1,0:T(8,128)S(1)}, u32[]{:S(2)}, u32[]{:S(2)}) async-start(f32[16,40,128]{2,1,0:T(8,128)} %broadcast_in_dim.22), calls=%async_computation.5 | async-start | bytes 655360 | tf_op jit(solution)/shard_map/products/all_to_all | solution.py:203
  131.4 5.9 %collective-permute-start.8 = (f32[16,40,128]{2,1,0:T(8,128)S(1)}, f32[16,40,128]{2,1,0:T(8,128)S(1)}, u32[]{:S(2)}, u32[]{:S(2)}) collective-permute-start(f32[16,40,128]{2,1,0:T(8,128)S(1)} %all-to-all-done.5.own_ref), channel_id=1, source_target_pairs={{0,4},{4,0},{1,5},{5,1},{2,6},{6,2},{3,7},{7,3},{8,12},{12,8},{9,1... | collective-permute-start | bytes 983048 | tf_op jit(solution)/shard_map/factor/ppermute | solution.py:211
  134.0 20.3 %all-to-all-start.6 = ((f32[4,64,128]{2,1,0:T(8,128)}), f32[4,64,128]{2,1,0:T(8,128)S(1)}, u32[]{:S(2)}, u32[]{:S(2)}) async-start(f32[4,64,128]{2,1,0:T(8,128)} %broadcast_in_dim.23), calls=%async_computation.6 | async-start | bytes 262144 | tf_op jit(solution)/shard_map/factor/all_to_all | solution.py:203
  148.2 10.7 %copy-start.3 = (f32[256,512]{1,0:T(8,128)}, f32[256,512]{1,0:T(8,128)S(1)}, u32[]{:S(2)}) copy-start(f32[256,512]{1,0:T(8,128)S(1)} %get-tuple-element.33.rest_ref) | copy-start | bytes 1572868
  155.2 16.0 %all-to-all-start.7 = ((f32[4,4,64,128]{3,2,1,0:T(8,128)}), f32[4,4,64,128]{3,2,1,0:T(8,128)S(1)}, u32[]{:S(2)}, u32[]{:S(2)}) async-start(f32[4,4,64,128]{3,2,1,0:T(8,128)} %broadcast_in_dim.24), calls=%async_computation.7 | async-start | bytes 1048576 | tf_op jit(solution)/shard_map/factor/all_to_all | solution.py:203
  158.9 1.0 copy-start.4
  170.4 0.8 copy-start.1
  171.2 3.8 %collective-permute-start.9 = (f32[16,4,16,128]{3,2,1,0:T(8,128)S(1)}, f32[16,4,16,128]{3,2,1,0:T(8,128)S(1)}, u32[]{:S(2)}, u32[]{:S(2)}) collective-permute-start(f32[16,4,16,128]{3,2,1,0:T(8,128)S(1)} %bitcast.25), channel_id=1, source_target_pairs={{0,4},{4,0},{1,5},{5,1},{2,6},{6,2},{3,7},{7,3},{8,12},{12,8},{9,1... | collective-permute-start | bytes 1572872 | tf_op jit(solution)/shard_map/right/ppermute | solution.py:211
  175.0 1.0 copy-start.2
  179.2 11.3 %all-to-all-start.8 = ((f32[16,1,512]{2,1,0:T(1,128)}), f32[16,1,512]{2,1,0:T(1,128)S(1)}, u32[]{:S(2)}, u32[]{:S(2)}) async-start(f32[16,1,512]{2,1,0:T(1,128)} %broadcast_in_dim.26), calls=%async_computation.8 | async-start | bytes 65536 | tf_op jit(solution)/shard_map/norms/all_to_all | solution.py:203

commit v4 on v3

--- a/solution.py
+++ b/solution.py
@@ -72,49 +72,48 @@
     return jnp.concatenate(done, axis=0)
 
 
-def eliminate(work, out, first, last, base):
-    size = work.shape[1]
-    for k in range(first, last):
-        a, b = k * EDGE, (k + 1) * EDGE
-        low, high = a - base, b - base
-        inv = invert_block(work[low:high, a:b])
-        if k:
-            out[low:high, :a] = dot(inv, work[low:high, :a], ((1,), (0,)))
-        out[low:high, a:b] = inv
-        if b < size:
-            out[low:high, b:] = jnp.zeros((EDGE, size - b), jnp.float32)
-            upper = dot(inv, work[low:high, b:], ((1,), (0,)))
-            full = jnp.concatenate([out[low:high, :b], upper], axis=1)
-            work[high:, a:b] = jnp.zeros((size - b, EDGE), jnp.float32)
-            work[high:, :] -= dot(upper, full, ((0,), (0,)))
-
-
 def upper_blocks(count):
     return [(k, j) for k in range(count) for j in range(k, count)]
 
 
-def factor_top(core_ref, own_ref, other_ref, top_ref, rest_ref, work, gram):
-    size = work.shape[0]
-    count = size // EDGE
+def factor_top(core_ref, own_ref, other_ref, top_ref, gram):
     slot = own_ref.shape[1]
     for refs, core in ((own_ref, core_ref[0]), (other_ref, 1 - core_ref[0])):
         for j in range(refs.shape[0]):
             gram[pl.ds(pl.multiple_of((2 * j + core) * slot, 8), slot), :] = refs[j]
-    work[...] = jnp.zeros_like(work)
-    for at, (k, j) in enumerate(upper_blocks(count)):
-        work[k * EDGE : (k + 1) * EDGE, j * EDGE : (j + 1) * EDGE] = gram[at * EDGE : (at + 1) * EDGE, :]
-    eliminate(work, top_ref, 0, count // 2, 0)
-    rest_ref[...] = work[size // 2 :, :]
-
-
-def factor_rest(rest_ref, top_ref, left_ref, low_ref, basis_ref, work):
-    size = work.shape[1]
-    half = size // 2
-    count = size // EDGE
-    work[...] = rest_ref[...]
-    eliminate(work, low_ref, count // 2, count, half)
-    basis_ref[:, :half] = dot(left_ref[:, :half], top_ref[:, :half], ((1,), (1,)))
-    basis_ref[:, half:] = dot(left_ref[...], low_ref[...], ((1,), (1,)))
+    g00, g01, g02, g03, g11, g12, g13, g22, g23, g33 = (
+        gram[at * EDGE : (at + 1) * EDGE, :] for at in range(len(upper_blocks(4)))
+    )
+    e1, e2, e3 = EDGE, 2 * EDGE, 3 * EDGE
+    inv = invert_block(g00)
+    upper = dot(inv, jnp.concatenate([g01, g02, g03], axis=1), ((1,), (0,)))
+    top_ref[:e1, :e1] = inv
+    top_ref[:e1, e1:e2] = jnp.zeros((e1, e1), jnp.float32)
+    top_ref[:e1, e2:] = upper[:, e1:]
+    less = dot(upper[:, :e1], jnp.concatenate([inv, upper], axis=1), ((0,), (0,)))
+    inv = invert_block(g11 - less[:, e1:e2])
+    top_ref[e1:e2, :e1] = dot(inv, -less[:, :e1], ((1,), (0,)))
+    top_ref[e1:e2, e1:e2] = inv
+    top_ref[e1:e2, e2:] = dot(inv, jnp.concatenate([g12, g13], axis=1) - less[:, e2:], ((1,), (0,)))
+    top_ref[e2:, :] = jnp.concatenate([g22, g23, g33, jnp.zeros_like(g33)], axis=1)
+
+
+def factor_rest(top_ref, left_ref, low_ref, basis_ref):
+    e1, e2, e3 = EDGE, 2 * EDGE, 3 * EDGE
+    less = dot(top_ref[:e2, e2:], top_ref[:e2, :], ((0,), (0,)))
+    inv = invert_block(top_ref[e2:, :e1] - less[:e1, e2:e3])
+    upper = dot(inv, top_ref[e2:, e1:e2] - less[:e1, e3:], ((1,), (0,)))
+    row = dot(inv, -less[:e1, :e2], ((1,), (0,)))
+    low_ref[:e1, :e2] = row
+    low_ref[:e1, e2:e3] = inv
+    low_ref[:e1, e3:] = jnp.zeros((e1, e1), jnp.float32)
+    last = dot(upper, jnp.concatenate([row, inv, upper], axis=1), ((0,), (0,)))
+    inv = invert_block(top_ref[e2:, e2:e3] - less[e1:, e3:] - last[:, e3:])
+    row = jnp.concatenate([-less[e1:, :e2] - last[:, :e2], -last[:, e2:e3]], axis=1)
+    low_ref[e1:, :e3] = dot(inv, row, ((1,), (0,)))
+    low_ref[e1:, e3:] = inv
+    basis_ref[:, :e2] = dot(left_ref[:, :e2], top_ref[:e2, :e2], ((1,), (1,)))
+    basis_ref[:, e2:] = dot(left_ref[...], low_ref[...], ((1,), (1,)))
 
 
 def left_part(core_ref, own_ref, other_ref, total_ref, out_ref, basis):
@@ -158,12 +157,12 @@
 
 
 def finish(core_ref, own_ref, other_ref, top_ref, low_ref, right_ref, squares_ref, prod):
-    half = top_ref.shape[0]
+    half = low_ref.shape[0]
     for refs, core in ((own_ref, core_ref[0]), (other_ref, 1 - core_ref[0])):
         at = pl.ds(pl.multiple_of(core * half, half), half)
         for j in range(refs.shape[1]):
             prod[at, j * EDGE : (j + 1) * EDGE] = refs[:, j].reshape(half, EDGE)
-    top = dot(top_ref[:, :half], prod[:half, :], ((1,), (0,)))
+    top = dot(top_ref[:half, :half], prod[:half, :], ((1,), (0,)))
     low = dot(low_ref[...], prod[...], ((1,), (0,)))
     right_ref[:half, :] = top
     right_ref[half:, :] = low
@@ -272,17 +271,17 @@
         prod, gram = lax.optimization_barrier((prod, gram))
     with jax.named_scope("factor"):
         half = (rank // 2, rank)
-        top, rest = call(
+        top = call(
             factor_top,
-            [half, half],
+            [(3 * EDGE, rank)],
             (core, gram, other_core(gram)),
             10**10,
-            [(rank, rank), (n_slots * slot, EDGE)],
+            [(n_slots * slot, EDGE)],
             1,
-        )
+        )[0]
         prod = share(prod, "far")
-        prod, rest = lax.optimization_barrier((prod, rest))
-        low, left_basis = call(factor_rest, [half, (rows, rank)], (rest, top, left), 10**10, [half])
+        prod, top = lax.optimization_barrier((prod, top))
+        low, left_basis = call(factor_rest, [half, (rows, rank)], (top, left), 10**10)
         prod = share(prod, "near")
         prod, low = lax.optimization_barrier((prod, low))
     with jax.named_scope("right"):

time: 212 us -> 211 us (level)
  the two profiles are of different devices: /device:TPU:32 before, /device:TPU:2 now
where the time goes in v4:
time: 211 us; the launch traced here: 210 us
  starting transfers between devices  77.8 us (37%)
  waiting for transfers between devices  60.9 us (29%)
  blocking collectives  31.8 us (15%)
  Pallas kernels  28.2 us (13%)
  local copies, waits for them, and re-layouts  7.34 us (3%)
  other arithmetic  2.72 us (1%)
    all_to_all x8, starting transfers between devices, swap(): return lax.all_to_all(x, axis, 0, 0, tiled=True)  50.9 us
    all_to_all x8, waiting for transfers between devices, swap(): return lax.all_to_all(x, axis, 0, 0, tiled=True)  42.3 us
    all_to_all x2, blocking collectives, swap(): return lax.all_to_all(x, axis, 0, 0, tiled=True)  31.8 us
    pallas_call x7, Pallas kernels, call(): pl.pallas_call(kernel, out_shape=[jax.ShapeDtypeStruct(s, t) for s, t in...  28.2 us
    ppermute x3, waiting for transfers between devices, per_device(): lax.ppermute(total, 'dp', turn(k))  14.3 us
    ppermute x3, starting transfers between devices, per_device(): lax.ppermute(column(grads[0], k), 'dp', turn(k))  9.88 us
    ppermute x3, starting transfers between devices, per_device(): lax.ppermute(total, 'dp', turn(k))  9.4 us
    ppermute x4, starting transfers between devices, other_core(): return lax.ppermute(x, 'core', [(0, 1), (1, 0)])  7.65 us
  transfers between devices with their start and end apart: 18, of which 14 were waited for; matrix products, arithmetic and copies ran while one was open for 1% of the time, Pallas kernels for 10%

profile of v4, /device:TPU:2, one launch (start us, length us, event | category | flops | bytes accessed | tf_op | source)
XLA Modules:
  0.0 209.7 jit_solution(1032271969660135468)
XLA Ops:
  0.7 0.8 copy-done
  1.5 0.7 broadcast_in_dim.18
  2.2 15.2 %all-to-all-start = ((bf16[16,16,512]{2,1,0:T(8,128)(2,1)}), bf16[16,16,512]{2,1,0:T(8,128)(2,1)S(1)}, u32[]{:S(2)}, u32[]{:S(2)}) async-start(bf16[16,16,512]{2,1,0:T(8,128)(2,1)} %broadcast_in_dim.18), calls=%async_computation | async-start | bytes 524288 | tf_op jit(solution)/shard_map/basis/all_to_all | solution.py:202
  17.5 3.4 %collective-permute-start.1 = (bf16[128,512]{1,0:T(8,128)(2,1)S(1)}, bf16[128,512]{1,0:T(8,128)(2,1)S(1)}, u32[]{:S(2)}, u32[]{:S(2)}) collective-permute-start(bf16[128,512]{1,0:T(8,128)(2,1)S(1)} %get-tuple-element.43), channel_id=1, source_target_pairs={{0,128},{128,256},{256,384},{384,0},{1,129},{129,257},{257,385},{3... | collective-permute-start | bytes 393224 | tf_op jit(solution)/shard_map/total/ppermute | solution.py:239
  20.9 2.4 %collective-permute-start.3 = (bf16[128,512]{1,0:T(8,128)(2,1)S(1)}, bf16[128,512]{1,0:T(8,128)(2,1)S(1)}, u32[]{:S(2)}, u32[]{:S(2)}) collective-permute-start(bf16[128,512]{1,0:T(8,128)(2,1)S(1)} %get-tuple-element.44), channel_id=1, source_target_pairs={{0,384},{128,0},{256,128},{384,256},{1,385},{129,1},{257,129},{385... | collective-permute-start | bytes 393224 | tf_op jit(solution)/shard_map/total/ppermute | solution.py:239
  23.4 4.0 %collective-permute-start.2 = (bf16[128,512]{1,0:T(8,128)(2,1)S(1)}, bf16[128,512]{1,0:T(8,128)(2,1)S(1)}, u32[]{:S(2)}, u32[]{:S(2)}) collective-permute-start(bf16[128,512]{1,0:T(8,128)(2,1)S(1)} %get-tuple-element.45), channel_id=1, source_target_pairs={{0,256},{128,384},{256,0},{384,128},{1,257},{129,385},{257,1},{385... | collective-permute-start | bytes 393224 | tf_op jit(solution)/shard_map/total/ppermute | solution.py:239
  27.4 8.4 %all-to-all-done.own_ref = bf16[16,16,512]{2,1,0:T(8,128)(2,1)S(1)} async-done(((bf16[16,16,512]{2,1,0:T(8,128)(2,1)}), bf16[16,16,512]{2,1,0:T(8,128)(2,1)S(1)}, u32[]{:S(2)}, u32[]{:S(2)}) %all-to-all-start) | async-done | bytes 262176 | tf_op jit(solution)/shard_map/basis/all_to_all | solution.py:202
  35.8 1.9 collective-permute-start
  37.7 1.0 fusion.2.total_ref.refs_0_
  39.9 14.4 %all_to_all.50 = f32[16,8,512]{2,1,0:T(8,128)S(1)} all-to-all(f32[16,8,512]{2,1,0:T(8,128)S(1)} %bitcast.29), channel_id=1, replica_groups=mesh['dp'=4,'far'=4,'near'=4,'core'=2,'tensor'=4] {'dp','tensor'}, dimensions={0} | all-to-all | bytes 524288 | tf_op jit(solution)/shard_map/left/all_to_all | solution.py:202
  54.3 0.7 broadcast_in_dim.19
  55.0 5.3 %all-to-all-start.2 = ((f32[16,8,512]{2,1,0:T(8,128)}), f32[16,8,512]{2,1,0:T(8,128)S(1)}, u32[]{:S(2)}, u32[]{:S(2)}) async-start(f32[16,8,512]{2,1,0:T(8,128)} %broadcast_in_dim.19), calls=%async_computation.2 | async-start | bytes 524288 | tf_op jit(solution)/shard_map/left/all_to_all | solution.py:202
  60.3 6.8 %all-to-all-done.2 = f32[16,8,512]{2,1,0:T(8,128)S(1)} async-done(((f32[16,8,512]{2,1,0:T(8,128)}), f32[16,8,512]{2,1,0:T(8,128)S(1)}, u32[]{:S(2)}, u32[]{:S(2)}) %all-to-all-start.2) | async-done | bytes 262176 | tf_op jit(solution)/shard_map/left/all_to_all | solution.py:202
  67.1 1.6 products.1
  68.8 1.9 collective-permute-start.4
  70.7 1.9 collective-permute-done.4
  72.7 0.9 pad_maximum_fusion
  73.6 4.4 %all-to-all-start.3 = ((f32[4,296,128]{2,1,0:T(8,128)}), f32[4,296,128]{2,1,0:T(8,128)S(1)}, u32[]{:S(2)}, u32[]{:S(2)}) async-start(f32[4,296,128]{2,1,0:T(8,128)} %pad_maximum_fusion), calls=%async_computation.3 | async-start | bytes 1212416 | tf_op jit(solution)/shard_map/products/all_to_all | solution.py:202
  78.0 3.7 %collective-permute-start.6 = (f32[128,512]{1,0:T(8,128)S(1)}, f32[128,512]{1,0:T(8,128)S(1)}, u32[]{:S(2)}, u32[]{:S(2)}) collective-permute-start(f32[128,512]{1,0:T(8,128)S(1)} %fusion.2.total_ref.refs_0_), channel_id=1, source_target_pairs={{0,384},{128,0},{256,128},{384,256},{1,385},{129,1},{257,129},{385... | collective-permute-start | bytes 786440 | tf_op jit(solution)/shard_map/totals/ppermute | solution.py:247
  81.6 2.2 %collective-permute-start.5 = (f32[128,512]{1,0:T(8,128)S(1)}, f32[128,512]{1,0:T(8,128)S(1)}, u32[]{:S(2)}, u32[]{:S(2)}) collective-permute-start(f32[128,512]{1,0:T(8,128)S(1)} %fusion.2.total_ref.refs_0_), channel_id=1, source_target_pairs={{0,128},{128,256},{256,384},{384,0},{1,129},{129,257},{257,385},{3... | collective-permute-start | bytes 786440 | tf_op jit(solution)/shard_map/totals/ppermute | solution.py:247
  83.8 4.1 %collective-permute-done.6.refs_3_ = f32[128,512]{1,0:T(8,128)S(1)} collective-permute-done((f32[128,512]{1,0:T(8,128)S(1)}, f32[128,512]{1,0:T(8,128)S(1)}, u32[]{:S(2)}, u32[]{:S(2)}) %collective-permute-start.6) | collective-permute-done | bytes 262176 | tf_op jit(solution)/shard_map/totals/ppermute | solution.py:247
  87.9 3.4 %collective-permute-done.5.refs_1_ = f32[128,512]{1,0:T(8,128)S(1)} collective-permute-done((f32[128,512]{1,0:T(8,128)S(1)}, f32[128,512]{1,0:T(8,128)S(1)}, u32[]{:S(2)}, u32[]{:S(2)}) %collective-permute-start.5) | collective-permute-done | bytes 262176 | tf_op jit(solution)/shard_map/totals/ppermute | solution.py:247
  91.3 3.2 %all-to-all-done.3 = f32[4,296,128]{2,1,0:T(8,128)S(1)} async-done(((f32[4,296,128]{2,1,0:T(8,128)}), f32[4,296,128]{2,1,0:T(8,128)S(1)}, u32[]{:S(2)}, u32[]{:S(2)}) %all-to-all-start.3) | async-done | bytes 606240 | tf_op jit(solution)/shard_map/products/all_to_all | solution.py:202
  95.3 5.4 %all-to-all-start.4 = ((f32[4,104,128]{2,1,0:T(8,128)}), f32[4,104,128]{2,1,0:T(8,128)S(1)}, u32[]{:S(2)}, u32[]{:S(2)}) async-start(f32[4,104,128]{2,1,0:T(8,128)} %pad_maximum_fusion.1), calls=%async_computation.4 | async-start | bytes 425984 | tf_op jit(solution)/shard_map/products/all_to_all | solution.py:202
  100.7 3.6 %collective-permute-start.7 = (f32[128,512]{1,0:T(8,128)S(1)}, f32[128,512]{1,0:T(8,128)S(1)}, u32[]{:S(2)}, u32[]{:S(2)}) collective-permute-start(f32[128,512]{1,0:T(8,128)S(1)} %fusion.2.total_ref.refs_0_), channel_id=1, source_target_pairs={{0,256},{128,384},{256,0},{384,128},{1,257},{129,385},{257,1},{385... | collective-permute-start | bytes 786440 | tf_op jit(solution)/shard_map/totals/ppermute | solution.py:247
  104.2 6.8 %collective-permute-done.7.refs_2_ = f32[128,512]{1,0:T(8,128)S(1)} collective-permute-done((f32[128,512]{1,0:T(8,128)S(1)}, f32[128,512]{1,0:T(8,128)S(1)}, u32[]{:S(2)}, u32[]{:S(2)}) %collective-permute-start.7) | collective-permute-done | bytes 262176 | tf_op jit(solution)/shard_map/totals/ppermute | solution.py:247
  111.1 6.2 %all-to-all-done.4 = f32[4,104,128]{2,1,0:T(8,128)S(1)} async-done(((f32[4,104,128]{2,1,0:T(8,128)}), f32[4,104,128]{2,1,0:T(8,128)S(1)}, u32[]{:S(2)}, u32[]{:S(2)}) %all-to-all-start.4) | async-done | bytes 213024 | tf_op jit(solution)/shard_map/products/all_to_all | solution.py:202
  117.4 0.7 broadcast_in_dim.22
  118.1 5.3 %all-to-all-start.5 = ((f32[16,40,128]{2,1,0:T(8,128)}), f32[16,40,128]{2,1,0:T(8,128)S(1)}, u32[]{:S(2)}, u32[]{:S(2)}) async-start(f32[16,40,128]{2,1,0:T(8,128)} %broadcast_in_dim.22), calls=%async_computation.5 | async-start | bytes 655360 | tf_op jit(solution)/shard_map/products/all_to_all | solution.py:202
  123.5 7.0 %all-to-all-done.5.own_ref = f32[16,40,128]{2,1,0:T(8,128)S(1)} async-done(((f32[16,40,128]{2,1,0:T(8,128)}), f32[16,40,128]{2,1,0:T(8,128)S(1)}, u32[]{:S(2)}, u32[]{:S(2)}) %all-to-all-start.5) | async-done | bytes 327712 | tf_op jit(solution)/shard_map/products/all_to_all | solution.py:202
  130.5 1.9 collective-permute-start.8
  133.1 5.5 %all-to-all-start.6 = ((f32[4,64,128]{2,1,0:T(8,128)}), f32[4,64,128]{2,1,0:T(8,128)S(1)}, u32[]{:S(2)}, u32[]{:S(2)}) async-start(f32[4,64,128]{2,1,0:T(8,128)} %broadcast_in_dim.23), calls=%async_computation.6 | async-start | bytes 262144 | tf_op jit(solution)/shard_map/factor/all_to_all | solution.py:202
  138.5 9.6 %factor_top.1.top_ref = f32[384,512]{1,0:T(8,128)S(1)} custom-call(s32[1]{0:T(128)} %bitcast.2.core_ref, f32[16,40,128]{2,1,0:T(8,128)S(1)} %all-to-all-done.5.own_ref, f32[16,40,128]{2,1,0:T(8,128)S(1)} %collective-permute-done.8.other_ref), custom_call_target="tpu_custom_call" | custom-call | flops 10000000000 | bytes 4194304 | tf_op jit(solution)/shard_map/factor/factor_top/pallas_call | solution.py:25
  148.1 0.9 copy-done.1
  149.0 3.1 %all-to-all-done.6 = f32[4,64,128]{2,1,0:T(8,128)S(1)} async-done(((f32[4,64,128]{2,1,0:T(8,128)}), f32[4,64,128]{2,1,0:T(8,128)S(1)}, u32[]{:S(2)}, u32[]{:S(2)}) %all-to-all-start.6) | async-done | bytes 131104 | tf_op jit(solution)/shard_map/factor/all_to_all | solution.py:202
  152.1 0.8 broadcast_in_dim.24
  153.0 4.3 %all-to-all-start.7 = ((f32[4,4,64,128]{3,2,1,0:T(8,128)}), f32[4,4,64,128]{3,2,1,0:T(8,128)S(1)}, u32[]{:S(2)}, u32[]{:S(2)}) async-start(f32[4,4,64,128]{3,2,1,0:T(8,128)} %broadcast_in_dim.24), calls=%async_computation.7 | async-start | bytes 1048576 | tf_op jit(solution)/shard_map/factor/all_to_all | solution.py:202
  157.3 11.4 %factor_rest.1 = (f32[256,512]{1,0:T(8,128)S(1)}, f32[128,512]{1,0:T(8,128)S(1)}) custom-call(f32[384,512]{1,0:T(8,128)S(1)} %copy-done.2, f32[128,512]{1,0:T(8,128)S(1)} %bitcast.28), custom_call_target="tpu_custom_call" | custom-call | flops 10000000000 | bytes 4194304 | tf_op jit(solution)/shard_map/factor/factor_rest/pallas_call | solution.py:25
  168.7 1.4 all-to-all-done.7
  170.1 1.9 collective-permute-start.9
  172.0 1.9 collective-permute-done.9.other_ref
  173.9 1.1 copy-done.3
  175.0 2.5 %finish.1 = (f32[512,512]{1,0:T(8,128)S(1)}, f32[8,512]{1,0:T(8,128)S(1)}) custom-call(s32[1]{0:T(128)} %bitcast.2.core_ref, f32[16,4,16,128]{3,2,1,0:T(8,128)S(1)} %bitcast.26, f32[16,4,16,128]{3,2,1,0:T(8,128)S(1)} %collective-permute-done.9.other_ref, f32[384,512]{1,0:T(8,128)S(1)} %copy-done.3, f32[256,512]{1,0:T(8,128)S(1)} %get-tuple-element.33.low_ref), custom_call_target="tpu_custom_call" | custom-call | flops 2000000000 | bytes 4194304 | tf_op jit(solution)/shard_map/right/finish/pallas_call | solution.py:25
  178.2 5.5 %all-to-all-start.8 = ((f32[16,1,512]{2,1,0:T(1,128)}), f32[16,1,512]{2,1,0:T(1,128)S(1)}, u32[]{:S(2)}, u32[]{:S(2)}) async-start(f32[16,1,512]{2,1,0:T(1,128)} %broadcast_in_dim.26), calls=%async_computation.8 | async-start | bytes 65536 | tf_op jit(solution)/shard_map/norms/all_to_all | solution.py:202
  183.6 6.2 %all-to-all-done.8 = f32[16,1,512]{2,1,0:T(1,128)S(1)} async-done(((f32[16,1,512]{2,1,0:T(1,128)}), f32[16,1,512]{2,1,0:T(1,128)S(1)}, u32[]{:S(2)}, u32[]{:S(2)}) %all-to-all-start.8) | async-done | bytes 32800 | tf_op jit(solution)/shard_map/norms/all_to_all | solution.py:202
  189.9 1.1 outputs.1
  191.0 17.4 %all_to_all.51.mixed_ref = bf16[4,272,512]{2,1,0:T(8,128)(2,1)S(1)} all-to-all(bf16[4,272,512]{2,1,0:T(8,128)(2,1)S(1)} %outputs.1), channel_id=1, replica_groups=mesh['dp'=4,'far'=4,'near'=4,'core'=2,'tensor'=4] {'dp'}, dimensions={0} | all-to-all | bytes 2228224 | tf_op jit(solution)/shard_map/outputs/all_to_all | solution.py:202
  208.4 1.3 merge.1
  (32 shorter events, 3.4 us)
Async XLA Ops:
  0.6 0.8 copy-start
  0.6 16.8 %copy-start.4 = (bf16[1,128,2048]{2,1,0:T(8,128)(2,1)S(1)}, bf16[1,128,2048]{2,1,0:T(8,128)(2,1)}, u32[]{:S(2)}) copy-start(bf16[1,128,2048]{2,1,0:T(8,128)(2,1)} %param.4) | copy-start | bytes 1572868
  2.2 33.6 %all-to-all-start = ((bf16[16,16,512]{2,1,0:T(8,128)(2,1)}), bf16[16,16,512]{2,1,0:T(8,128)(2,1)S(1)}, u32[]{:S(2)}, u32[]{:S(2)}) async-start(bf16[16,16,512]{2,1,0:T(8,128)(2,1)} %broadcast_in_dim.18), calls=%async_computation | async-start | bytes 524288 | tf_op jit(solution)/shard_map/basis/all_to_all | solution.py:202
  17.5 20.2 %collective-permute-start.1 = (bf16[128,512]{1,0:T(8,128)(2,1)S(1)}, bf16[128,512]{1,0:T(8,128)(2,1)S(1)}, u32[]{:S(2)}, u32[]{:S(2)}) collective-permute-start(bf16[128,512]{1,0:T(8,128)(2,1)S(1)} %get-tuple-element.43), channel_id=1, source_target_pairs={{0,128},{128,256},{256,384},{384,0},{1,129},{129,257},{257,385},{3... | collective-permute-start | bytes 393224 | tf_op jit(solution)/shard_map/total/ppermute | solution.py:239
  20.9 16.8 %collective-permute-start.3 = (bf16[128,512]{1,0:T(8,128)(2,1)S(1)}, bf16[128,512]{1,0:T(8,128)(2,1)S(1)}, u32[]{:S(2)}, u32[]{:S(2)}) collective-permute-start(bf16[128,512]{1,0:T(8,128)(2,1)S(1)} %get-tuple-element.44), channel_id=1, source_target_pairs={{0,384},{128,0},{256,128},{384,256},{1,385},{129,1},{257,129},{385... | collective-permute-start | bytes 393224 | tf_op jit(solution)/shard_map/total/ppermute | solution.py:239
  23.4 14.4 %collective-permute-start.2 = (bf16[128,512]{1,0:T(8,128)(2,1)S(1)}, bf16[128,512]{1,0:T(8,128)(2,1)S(1)}, u32[]{:S(2)}, u32[]{:S(2)}) collective-permute-start(bf16[128,512]{1,0:T(8,128)(2,1)S(1)} %get-tuple-element.45), channel_id=1, source_target_pairs={{0,256},{128,384},{256,0},{384,128},{1,257},{129,385},{257,1},{385... | collective-permute-start | bytes 393224 | tf_op jit(solution)/shard_map/total/ppermute | solution.py:239
  35.8 3.4 %collective-permute-start = (bf16[16,16,512]{2,1,0:T(8,128)(2,1)S(1)}, bf16[16,16,512]{2,1,0:T(8,128)(2,1)S(1)}, u32[]{:S(2)}, u32[]{:S(2)}) collective-permute-start(bf16[16,16,512]{2,1,0:T(8,128)(2,1)S(1)} %all-to-all-done.own_ref), channel_id=1, source_target_pairs={{0,4},{4,0},{1,5},{5,1},{2,6},{6,2},{3,7},{7,3},{8,12},{12,8},{9,1... | collective-permute-start | bytes 786440 | tf_op jit(solution)/shard_map/basis/ppermute | solution.py:210
  55.0 12.1 %all-to-all-start.2 = ((f32[16,8,512]{2,1,0:T(8,128)}), f32[16,8,512]{2,1,0:T(8,128)S(1)}, u32[]{:S(2)}, u32[]{:S(2)}) async-start(f32[16,8,512]{2,1,0:T(8,128)} %broadcast_in_dim.19), calls=%async_computation.2 | async-start | bytes 524288 | tf_op jit(solution)/shard_map/left/all_to_all | solution.py:202
  68.8 3.8 %collective-permute-start.4 = (f32[1064,128]{1,0:T(8,128)S(1)}, f32[1064,128]{1,0:T(8,128)S(1)}, u32[]{:S(2)}, u32[]{:S(2)}) collective-permute-start(f32[1064,128]{1,0:T(8,128)S(1)} %get-tuple-element.24), channel_id=1, source_target_pairs={{0,4},{4,0},{1,5},{5,1},{2,6},{6,2},{3,7},{7,3},{8,12},{12,8},{9,1... | collective-permute-start | bytes 1634312 | tf_op jit(solution)/shard_map/products/ppermute | solution.py:210
  73.6 20.9 %all-to-all-start.3 = ((f32[4,296,128]{2,1,0:T(8,128)}), f32[4,296,128]{2,1,0:T(8,128)S(1)}, u32[]{:S(2)}, u32[]{:S(2)}) async-start(f32[4,296,128]{2,1,0:T(8,128)} %pad_maximum_fusion), calls=%async_computation.3 | async-start | bytes 1212416 | tf_op jit(solution)/shard_map/products/all_to_all | solution.py:202
  78.0 9.9 %collective-permute-start.6 = (f32[128,512]{1,0:T(8,128)S(1)}, f32[128,512]{1,0:T(8,128)S(1)}, u32[]{:S(2)}, u32[]{:S(2)}) collective-permute-start(f32[128,512]{1,0:T(8,128)S(1)} %fusion.2.total_ref.refs_0_), channel_id=1, source_target_pairs={{0,384},{128,0},{256,128},{384,256},{1,385},{129,1},{257,129},{385... | collective-permute-start | bytes 786440 | tf_op jit(solution)/shard_map/totals/ppermute | solution.py:247
  81.6 9.7 %collective-permute-start.5 = (f32[128,512]{1,0:T(8,128)S(1)}, f32[128,512]{1,0:T(8,128)S(1)}, u32[]{:S(2)}, u32[]{:S(2)}) collective-permute-start(f32[128,512]{1,0:T(8,128)S(1)} %fusion.2.total_ref.refs_0_), channel_id=1, source_target_pairs={{0,128},{128,256},{256,384},{384,0},{1,129},{129,257},{257,385},{3... | collective-permute-start | bytes 786440 | tf_op jit(solution)/shard_map/totals/ppermute | solution.py:247
  95.3 22.0 %all-to-all-start.4 = ((f32[4,104,128]{2,1,0:T(8,128)}), f32[4,104,128]{2,1,0:T(8,128)S(1)}, u32[]{:S(2)}, u32[]{:S(2)}) async-start(f32[4,104,128]{2,1,0:T(8,128)} %pad_maximum_fusion.1), calls=%async_computation.4 | async-start | bytes 425984 | tf_op jit(solution)/shard_map/products/all_to_all | solution.py:202
  100.7 10.4 %collective-permute-start.7 = (f32[128,512]{1,0:T(8,128)S(1)}, f32[128,512]{1,0:T(8,128)S(1)}, u32[]{:S(2)}, u32[]{:S(2)}) collective-permute-start(f32[128,512]{1,0:T(8,128)S(1)} %fusion.2.total_ref.refs_0_), channel_id=1, source_target_pairs={{0,256},{128,384},{256,0},{384,128},{1,257},{129,385},{257,1},{385... | collective-permute-start | bytes 786440 | tf_op jit(solution)/shard_map/totals/ppermute | solution.py:247
  118.1 12.4 %all-to-all-start.5 = ((f32[16,40,128]{2,1,0:T(8,128)}), f32[16,40,128]{2,1,0:T(8,128)S(1)}, u32[]{:S(2)}, u32[]{:S(2)}) async-start(f32[16,40,128]{2,1,0:T(8,128)} %broadcast_in_dim.22), calls=%async_computation.5 | async-start | bytes 655360 | tf_op jit(solution)/shard_map/products/all_to_all | solution.py:202
  130.5 8.1 %collective-permute-start.8 = (f32[16,40,128]{2,1,0:T(8,128)S(1)}, f32[16,40,128]{2,1,0:T(8,128)S(1)}, u32[]{:S(2)}, u32[]{:S(2)}) collective-permute-start(f32[16,40,128]{2,1,0:T(8,128)S(1)} %all-to-all-done.5.own_ref), channel_id=1, source_target_pairs={{0,4},{4,0},{1,5},{5,1},{2,6},{6,2},{3,7},{7,3},{8,12},{12,8},{9,1... | collective-permute-start | bytes 983048 | tf_op jit(solution)/shard_map/factor/ppermute | solution.py:210
  133.1 19.1 %all-to-all-start.6 = ((f32[4,64,128]{2,1,0:T(8,128)}), f32[4,64,128]{2,1,0:T(8,128)S(1)}, u32[]{:S(2)}, u32[]{:S(2)}) async-start(f32[4,64,128]{2,1,0:T(8,128)} %broadcast_in_dim.23), calls=%async_computation.6 | async-start | bytes 262144 | tf_op jit(solution)/shard_map/factor/all_to_all | solution.py:202
  148.1 0.9 copy-start.1
  152.1 5.2 %copy-start.2 = (f32[384,512]{1,0:T(8,128)S(1)}, f32[384,512]{1,0:T(8,128)}, u32[]{:S(2)}) copy-start(f32[384,512]{1,0:T(8,128)} %copy-done.1) | copy-start | bytes 2359300
  153.0 17.1 %all-to-all-start.7 = ((f32[4,4,64,128]{3,2,1,0:T(8,128)}), f32[4,4,64,128]{3,2,1,0:T(8,128)S(1)}, u32[]{:S(2)}, u32[]{:S(2)}) async-start(f32[4,4,64,128]{3,2,1,0:T(8,128)} %broadcast_in_dim.24), calls=%async_computation.7 | async-start | bytes 1048576 | tf_op jit(solution)/shard_map/factor/all_to_all | solution.py:202
  170.1 3.8 %collective-permute-start.9 = (f32[16,4,16,128]{3,2,1,0:T(8,128)S(1)}, f32[16,4,16,128]{3,2,1,0:T(8,128)S(1)}, u32[]{:S(2)}, u32[]{:S(2)}) collective-permute-start(f32[16,4,16,128]{3,2,1,0:T(8,128)S(1)} %bitcast.25), channel_id=1, source_target_pairs={{0,4},{4,0},{1,5},{5,1},{2,6},{6,2},{3,7},{7,3},{8,12},{12,8},{9,1... | collective-permute-start | bytes 1572872 | tf_op jit(solution)/shard_map/right/ppermute | solution.py:210
  173.9 1.1 copy-start.3
  178.2 11.7 %all-to-all-start.8 = ((f32[16,1,512]{2,1,0:T(1,128)}), f32[16,1,512]{2,1,0:T(1,128)S(1)}, u32[]{:S(2)}, u32[]{:S(2)}) async-start(f32[16,1,512]{2,1,0:T(1,128)} %broadcast_in_dim.26), calls=%async_computation.8 | async-start | bytes 65536 | tf_op jit(solution)/shard_map/norms/all_to_all | solution.py:202

commit v5 on v4

--- a/solution.py
+++ b/solution.py
@@ -116,7 +116,12 @@
     basis_ref[:, e2:] = dot(left_ref[...], low_ref[...], ((1,), (1,)))
 
 
-def left_part(core_ref, own_ref, other_ref, total_ref, out_ref, basis):
+def left_part(core_ref, own_ref, other_ref, momentum_ref, *refs):
+    grads, (out_ref, total_ref, basis) = refs[:-3], refs[-3:]
+    summed = grads[0][...].astype(jnp.float32)
+    for ref in grads[1:]:
+        summed += ref[...].astype(jnp.float32)
+    total_ref[...] = momentum_ref[...] + summed
     count, ranks, _ = own_ref.shape
     for refs, core in ((own_ref, core_ref[0]), (other_ref, 1 - core_ref[0])):
         for z in range(count):
@@ -231,16 +236,22 @@
     with jax.named_scope("basis"):
         mine = lax.dynamic_slice_in_dim(right_basis.T, d * cols, cols, 1)
         part = share(mine, ("far", "near"))
-        other = other_core(part)
     with jax.named_scope("total"):
         def column(x, k):
             return lax.dynamic_slice_in_dim(x, (d + k) % n_dp * cols, cols, 1)
 
         blocks = [lax.ppermute(column(grads[0], k), "dp", turn(k)) for k in range(1, n_dp)]
-        total = sum((b.astype(jnp.float32) for b in blocks), column(grads[0], 0).astype(jnp.float32))
-        total = column(momentum, 0) + total
+        part, *blocks = lax.optimization_barrier((part, *blocks, column(momentum, 0)))
+        other = other_core(part)
     with jax.named_scope("left"):
-        partial = call(left_part, [(rows, rank)], (core, part, other, total), 10**9, [((rank, cols), jnp.bfloat16)], 1)[0]
+        partial, total = call(
+            left_part,
+            [(rows, rank), (rows, cols)],
+            (core, part, other, blocks[-1], column(grads[0], 0), *blocks[:-1]),
+            10**9,
+            [((rank, cols), jnp.bfloat16)],
+            1,
+        )
         partial = swap(partial.reshape(n_dp * n_tensor, rows // (n_dp * n_tensor), rank), BOTH)
         left = share(jnp.sum(partial, axis=0), BOTH).reshape(rows, rank)
     with jax.named_scope("totals"):

time: 211 us -> 219 us (1.038)
  the two profiles are of different devices: /device:TPU:2 before, /device:TPU:32 now
where the time goes in v5:
time: 219 us; the launch traced here: 218 us
  starting transfers between devices  79.4 us (36%)
  waiting for transfers between devices  61.6 us (28%)
  blocking collectives  33 us (15%)
  Pallas kernels  28.2 us (13%)
  local copies, waits for them, and re-layouts  12.6 us (6%)
    all_to_all x8, starting transfers between devices, swap(): return lax.all_to_all(x, axis, 0, 0, tiled=True)  51 us
    all_to_all x8, waiting for transfers between devices, swap(): return lax.all_to_all(x, axis, 0, 0, tiled=True)  38.8 us
    all_to_all x2, blocking collectives, swap(): return lax.all_to_all(x, axis, 0, 0, tiled=True)  33 us
    pallas_call x7, Pallas kernels, call(): pl.pallas_call(kernel, out_shape=[jax.ShapeDtypeStruct(s, t) for s, t in...  28.2 us
    ppermute x3, waiting for transfers between devices, per_device(): lax.ppermute(total, 'dp', turn(k))  15.1 us
    ppermute x3, starting transfers between devices, per_device(): lax.ppermute(column(grads[0], k), 'dp', turn(k))  12 us
    ppermute x3, starting transfers between devices, per_device(): lax.ppermute(total, 'dp', turn(k))  8.74 us
    ppermute x4, starting transfers between devices, other_core(): return lax.ppermute(x, 'core', [(0, 1), (1, 0)])  7.65 us
  transfers between devices with their start and end apart: 18, of which 14 were waited for; matrix products, arithmetic and copies ran while one was open for 0% of the time, Pallas kernels for 10%

profile of v5, /device:TPU:32, one launch (start us, length us, event | category | flops | bytes accessed | tf_op | source)
XLA Modules:
  0.0 217.5 jit_solution(162077534062462644)
XLA Ops:
  2.2 15.2 %all-to-all-start = ((bf16[16,16,512]{2,1,0:T(8,128)(2,1)}), bf16[16,16,512]{2,1,0:T(8,128)(2,1)S(1)}, u32[]{:S(2)}, u32[]{:S(2)}) async-start(bf16[16,16,512]{2,1,0:T(8,128)(2,1)} %broadcast_in_dim.18), calls=%async_computation | async-start | bytes 524288 | tf_op jit(solution)/shard_map/basis/all_to_all | solution.py:207
  17.5 4.9 %collective-permute-start.1 = (bf16[128,512]{1,0:T(8,128)(2,1)S(1)}, bf16[128,512]{1,0:T(8,128)(2,1)S(1)}, u32[]{:S(2)}, u32[]{:S(2)}) collective-permute-start(bf16[128,512]{1,0:T(8,128)(2,1)S(1)} %get-tuple-element.58), channel_id=1, source_target_pairs={{0,256},{128,384},{256,0},{384,128},{1,257},{129,385},{257,1},{385... | collective-permute-start | bytes 393224 | tf_op jit(solution)/shard_map/total/ppermute | solution.py:243
  22.4 2.5 %collective-permute-start = (bf16[128,512]{1,0:T(8,128)(2,1)S(1)}, bf16[128,512]{1,0:T(8,128)(2,1)S(1)}, u32[]{:S(2)}, u32[]{:S(2)}) collective-permute-start(bf16[128,512]{1,0:T(8,128)(2,1)S(1)} %get-tuple-element.59), channel_id=1, source_target_pairs={{0,128},{128,256},{256,384},{384,0},{1,129},{129,257},{257,385},{3... | collective-permute-start | bytes 393224 | tf_op jit(solution)/shard_map/total/ppermute | solution.py:243
  25.0 4.6 %collective-permute-start.2 = (bf16[128,512]{1,0:T(8,128)(2,1)S(1)}, bf16[128,512]{1,0:T(8,128)(2,1)S(1)}, u32[]{:S(2)}, u32[]{:S(2)}) collective-permute-start(bf16[128,512]{1,0:T(8,128)(2,1)S(1)} %get-tuple-element.60), channel_id=1, source_target_pairs={{0,384},{128,0},{256,128},{384,256},{1,385},{129,1},{257,129},{385... | collective-permute-start | bytes 393224 | tf_op jit(solution)/shard_map/total/ppermute | solution.py:243
  29.6 0.9 collective-permute-done.refs_1_
  30.5 1.5 collective-permute-done.2.refs_3_
  32.0 3.3 %all-to-all-done.own_ref = bf16[16,16,512]{2,1,0:T(8,128)(2,1)S(1)} async-done(((bf16[16,16,512]{2,1,0:T(8,128)(2,1)}), bf16[16,16,512]{2,1,0:T(8,128)(2,1)S(1)}, u32[]{:S(2)}, u32[]{:S(2)}) %all-to-all-start) | async-done | bytes 262176 | tf_op jit(solution)/shard_map/basis/all_to_all | solution.py:207
  35.3 1.9 collective-permute-start.3
  37.3 1.5 collective-permute-done.3.other_ref
  39.5 15.6 %all_to_all.50 = f32[16,8,512]{2,1,0:T(8,128)S(1)} all-to-all(f32[16,8,512]{2,1,0:T(8,128)S(1)} %bitcast.28), channel_id=1, replica_groups=mesh['dp'=4,'far'=4,'near'=4,'core'=2,'tensor'=4] {'dp','tensor'}, dimensions={0} | all-to-all | bytes 524288 | tf_op jit(solution)/shard_map/left/all_to_all | solution.py:207
  55.9 3.6 %all-to-all-start.2 = ((f32[16,8,512]{2,1,0:T(8,128)}), f32[16,8,512]{2,1,0:T(8,128)S(1)}, u32[]{:S(2)}, u32[]{:S(2)}) async-start(f32[16,8,512]{2,1,0:T(8,128)} %broadcast_in_dim.19), calls=%async_computation.2 | async-start | bytes 524288 | tf_op jit(solution)/shard_map/left/all_to_all | solution.py:207
  59.5 8.5 %all-to-all-done.2 = f32[16,8,512]{2,1,0:T(8,128)S(1)} async-done(((f32[16,8,512]{2,1,0:T(8,128)}), f32[16,8,512]{2,1,0:T(8,128)S(1)}, u32[]{:S(2)}, u32[]{:S(2)}) %all-to-all-start.2) | async-done | bytes 262176 | tf_op jit(solution)/shard_map/left/all_to_all | solution.py:207
  68.0 1.6 products.1
  69.6 1.9 collective-permute-start.4
  71.5 1.9 collective-permute-done.4
  73.5 0.9 pad_maximum_fusion
  74.4 4.9 %all-to-all-start.3 = ((f32[4,296,128]{2,1,0:T(8,128)}), f32[4,296,128]{2,1,0:T(8,128)S(1)}, u32[]{:S(2)}, u32[]{:S(2)}) async-start(f32[4,296,128]{2,1,0:T(8,128)} %pad_maximum_fusion), calls=%async_computation.3 | async-start | bytes 1212416 | tf_op jit(solution)/shard_map/products/all_to_all | solution.py:207
  79.3 3.0 %collective-permute-start.6 = (f32[128,512]{1,0:T(8,128)S(1)}, f32[128,512]{1,0:T(8,128)S(1)}, u32[]{:S(2)}, u32[]{:S(2)}) collective-permute-start(f32[128,512]{1,0:T(8,128)S(1)} %get-tuple-element.36.total_ref.refs_0_), channel_id=1, source_target_pairs={{0,384},{128,0},{256,128},{384,256},{1,385},{129,1},{257,129},{385... | collective-permute-start | bytes 786440 | tf_op jit(solution)/shard_map/totals/ppermute | solution.py:258
  82.3 2.9 %collective-permute-start.5 = (f32[128,512]{1,0:T(8,128)S(1)}, f32[128,512]{1,0:T(8,128)S(1)}, u32[]{:S(2)}, u32[]{:S(2)}) collective-permute-start(f32[128,512]{1,0:T(8,128)S(1)} %get-tuple-element.36.total_ref.refs_0_), channel_id=1, source_target_pairs={{0,128},{128,256},{256,384},{384,0},{1,129},{129,257},{257,385},{3... | collective-permute-start | bytes 786440 | tf_op jit(solution)/shard_map/totals/ppermute | solution.py:258
  85.2 3.8 %collective-permute-done.6.refs_3_ = f32[128,512]{1,0:T(8,128)S(1)} collective-permute-done((f32[128,512]{1,0:T(8,128)S(1)}, f32[128,512]{1,0:T(8,128)S(1)}, u32[]{:S(2)}, u32[]{:S(2)}) %collective-permute-start.6) | collective-permute-done | bytes 262176 | tf_op jit(solution)/shard_map/totals/ppermute | solution.py:258
  89.0 3.9 %collective-permute-done.5.refs_1_ = f32[128,512]{1,0:T(8,128)S(1)} collective-permute-done((f32[128,512]{1,0:T(8,128)S(1)}, f32[128,512]{1,0:T(8,128)S(1)}, u32[]{:S(2)}, u32[]{:S(2)}) %collective-permute-start.5) | collective-permute-done | bytes 262176 | tf_op jit(solution)/shard_map/totals/ppermute | solution.py:258
  93.7 8.1 %all-to-all-start.4 = ((f32[4,104,128]{2,1,0:T(8,128)}), f32[4,104,128]{2,1,0:T(8,128)S(1)}, u32[]{:S(2)}, u32[]{:S(2)}) async-start(f32[4,104,128]{2,1,0:T(8,128)} %pad_maximum_fusion.1), calls=%async_computation.4 | async-start | bytes 425984 | tf_op jit(solution)/shard_map/products/all_to_all | solution.py:207
  101.8 2.9 %collective-permute-start.7 = (f32[128,512]{1,0:T(8,128)S(1)}, f32[128,512]{1,0:T(8,128)S(1)}, u32[]{:S(2)}, u32[]{:S(2)}) collective-permute-start(f32[128,512]{1,0:T(8,128)S(1)} %get-tuple-element.36.total_ref.refs_0_), channel_id=1, source_target_pairs={{0,256},{128,384},{256,0},{384,128},{1,257},{129,385},{257,1},{385... | collective-permute-start | bytes 786440 | tf_op jit(solution)/shard_map/totals/ppermute | solution.py:258
  104.7 7.4 %collective-permute-done.7.refs_2_ = f32[128,512]{1,0:T(8,128)S(1)} collective-permute-done((f32[128,512]{1,0:T(8,128)S(1)}, f32[128,512]{1,0:T(8,128)S(1)}, u32[]{:S(2)}, u32[]{:S(2)}) %collective-permute-start.7) | collective-permute-done | bytes 262176 | tf_op jit(solution)/shard_map/totals/ppermute | solution.py:258
  112.1 6.6 %all-to-all-done.4 = f32[4,104,128]{2,1,0:T(8,128)S(1)} async-done(((f32[4,104,128]{2,1,0:T(8,128)}), f32[4,104,128]{2,1,0:T(8,128)S(1)}, u32[]{:S(2)}, u32[]{:S(2)}) %all-to-all-start.4) | async-done | bytes 213024 | tf_op jit(solution)/shard_map/products/all_to_all | solution.py:207
  119.5 3.6 %all-to-all-start.5 = ((f32[16,40,128]{2,1,0:T(8,128)}), f32[16,40,128]{2,1,0:T(8,128)S(1)}, u32[]{:S(2)}, u32[]{:S(2)}) async-start(f32[16,40,128]{2,1,0:T(8,128)} %broadcast_in_dim.22), calls=%async_computation.5 | async-start | bytes 655360 | tf_op jit(solution)/shard_map/products/all_to_all | solution.py:207
  123.2 8.8 %all-to-all-done.5.own_ref = f32[16,40,128]{2,1,0:T(8,128)S(1)} async-done(((f32[16,40,128]{2,1,0:T(8,128)}), f32[16,40,128]{2,1,0:T(8,128)S(1)}, u32[]{:S(2)}, u32[]{:S(2)}) %all-to-all-start.5) | async-done | bytes 327712 | tf_op jit(solution)/shard_map/products/all_to_all | solution.py:207
  132.0 1.9 collective-permute-start.8
  134.6 5.1 %all-to-all-start.6 = ((f32[4,64,128]{2,1,0:T(8,128)}), f32[4,64,128]{2,1,0:T(8,128)S(1)}, u32[]{:S(2)}, u32[]{:S(2)}) async-start(f32[4,64,128]{2,1,0:T(8,128)} %broadcast_in_dim.23), calls=%async_computation.6 | async-start | bytes 262144 | tf_op jit(solution)/shard_map/factor/all_to_all | solution.py:207
  139.7 9.6 %factor_top.1.top_ref = f32[384,512]{1,0:T(8,128)S(1)} custom-call(s32[1]{0:T(128)} %bitcast.2.core_ref, f32[16,40,128]{2,1,0:T(8,128)S(1)} %all-to-all-done.5.own_ref, f32[16,40,128]{2,1,0:T(8,128)S(1)} %collective-permute-done.8.other_ref), custom_call_target="tpu_custom_call" | custom-call | flops 10000000000 | bytes 4194304 | tf_op jit(solution)/shard_map/factor/factor_top/pallas_call | solution.py:25
  149.3 0.9 copy-done.3
  150.2 3.9 %all-to-all-done.6 = f32[4,64,128]{2,1,0:T(8,128)S(1)} async-done(((f32[4,64,128]{2,1,0:T(8,128)}), f32[4,64,128]{2,1,0:T(8,128)S(1)}, u32[]{:S(2)}, u32[]{:S(2)}) %all-to-all-start.6) | async-done | bytes 131104 | tf_op jit(solution)/shard_map/factor/all_to_all | solution.py:207
  154.1 0.8 broadcast_in_dim.24
  155.0 6.7 %all-to-all-start.7 = ((f32[4,4,64,128]{3,2,1,0:T(8,128)}), f32[4,4,64,128]{3,2,1,0:T(8,128)S(1)}, u32[]{:S(2)}, u32[]{:S(2)}) async-start(f32[4,4,64,128]{3,2,1,0:T(8,128)} %broadcast_in_dim.24), calls=%async_computation.7 | async-start | bytes 1048576 | tf_op jit(solution)/shard_map/factor/all_to_all | solution.py:207
  161.7 1.1 copy-done.4
  162.8 11.4 %factor_rest.1 = (f32[256,512]{1,0:T(8,128)S(1)}, f32[128,512]{1,0:T(8,128)S(1)}) custom-call(f32[384,512]{1,0:T(8,128)S(1)} %copy-done.4, f32[128,512]{1,0:T(8,128)S(1)} %bitcast.27), custom_call_target="tpu_custom_call" | custom-call | flops 10000000000 | bytes 4194304 | tf_op jit(solution)/shard_map/factor/factor_rest/pallas_call | solution.py:25
  175.1 1.9 collective-permute-start.9
  177.0 1.9 collective-permute-done.9.other_ref
  178.9 1.1 copy-done.5
  180.0 1.0 copy-done.7
  181.0 2.5 %finish.1 = (f32[512,512]{1,0:T(8,128)S(1)}, f32[8,512]{1,0:T(8,128)S(1)}) custom-call(s32[1]{0:T(128)} %bitcast.2.core_ref, f32[16,4,16,128]{3,2,1,0:T(8,128)S(1)} %bitcast.25, f32[16,4,16,128]{3,2,1,0:T(8,128)S(1)} %collective-permute-done.9.other_ref, f32[384,512]{1,0:T(8,128)S(1)} %copy-done.5, f32[256,512]{1,0:T(8,128)S(1)} %copy-done.7), custom_call_target="tpu_custom_call" | custom-call | flops 2000000000 | bytes 4194304 | tf_op jit(solution)/shard_map/right/finish/pallas_call | solution.py:25
  183.5 1.0 copy-done.1
  185.2 3.7 %all-to-all-start.8 = ((f32[16,1,512]{2,1,0:T(1,128)}), f32[16,1,512]{2,1,0:T(1,128)S(1)}, u32[]{:S(2)}, u32[]{:S(2)}) async-start(f32[16,1,512]{2,1,0:T(1,128)} %broadcast_in_dim.26), calls=%async_computation.8 | async-start | bytes 65536 | tf_op jit(solution)/shard_map/norms/all_to_all | solution.py:207
  188.9 7.6 %all-to-all-done.8 = f32[16,1,512]{2,1,0:T(1,128)S(1)} async-done(((f32[16,1,512]{2,1,0:T(1,128)}), f32[16,1,512]{2,1,0:T(1,128)S(1)}, u32[]{:S(2)}, u32[]{:S(2)}) %all-to-all-start.8) | async-done | bytes 32800 | tf_op jit(solution)/shard_map/norms/all_to_all | solution.py:207
  196.5 1.2 copy-done.2
  197.7 1.1 outputs.1
  198.9 17.4 %all_to_all.51.mixed_ref = bf16[4,272,512]{2,1,0:T(8,128)(2,1)S(1)} all-to-all(bf16[4,272,512]{2,1,0:T(8,128)(2,1)S(1)} %outputs.1), channel_id=1, replica_groups=mesh['dp'=4,'far'=4,'near'=4,'core'=2,'tensor'=4] {'dp'}, dimensions={0} | all-to-all | bytes 2228224 | tf_op jit(solution)/shard_map/outputs/all_to_all | solution.py:207
  216.2 1.3 merge.1
  (40 shorter events, 6.9 us)
Async XLA Ops:
  0.6 28.9 %copy-start = (f32[128,2048]{1,0:T(8,128)S(1)}, f32[128,2048]{1,0:T(8,128)}, u32[]{:S(2)}) copy-start(f32[128,2048]{1,0:T(8,128)} %param.3) | copy-start | bytes 3145732
  0.6 16.8 %copy-start.8 = (bf16[1,128,2048]{2,1,0:T(8,128)(2,1)S(1)}, bf16[1,128,2048]{2,1,0:T(8,128)(2,1)}, u32[]{:S(2)}) copy-start(bf16[1,128,2048]{2,1,0:T(8,128)(2,1)} %param.4) | copy-start | bytes 1572868
  2.2 33.1 %all-to-all-start = ((bf16[16,16,512]{2,1,0:T(8,128)(2,1)}), bf16[16,16,512]{2,1,0:T(8,128)(2,1)S(1)}, u32[]{:S(2)}, u32[]{:S(2)}) async-start(bf16[16,16,512]{2,1,0:T(8,128)(2,1)} %broadcast_in_dim.18), calls=%async_computation | async-start | bytes 524288 | tf_op jit(solution)/shard_map/basis/all_to_all | solution.py:207
  17.5 12.1 %collective-permute-start.1 = (bf16[128,512]{1,0:T(8,128)(2,1)S(1)}, bf16[128,512]{1,0:T(8,128)(2,1)S(1)}, u32[]{:S(2)}, u32[]{:S(2)}) collective-permute-start(bf16[128,512]{1,0:T(8,128)(2,1)S(1)} %get-tuple-element.58), channel_id=1, source_target_pairs={{0,256},{128,384},{256,0},{384,128},{1,257},{129,385},{257,1},{385... | collective-permute-start | bytes 393224 | tf_op jit(solution)/shard_map/total/ppermute | solution.py:243
  22.4 8.1 %collective-permute-start = (bf16[128,512]{1,0:T(8,128)(2,1)S(1)}, bf16[128,512]{1,0:T(8,128)(2,1)S(1)}, u32[]{:S(2)}, u32[]{:S(2)}) collective-permute-start(bf16[128,512]{1,0:T(8,128)(2,1)S(1)} %get-tuple-element.59), channel_id=1, source_target_pairs={{0,128},{128,256},{256,384},{384,0},{1,129},{129,257},{257,385},{3... | collective-permute-start | bytes 393224 | tf_op jit(solution)/shard_map/total/ppermute | solution.py:243
  25.0 7.1 %collective-permute-start.2 = (bf16[128,512]{1,0:T(8,128)(2,1)S(1)}, bf16[128,512]{1,0:T(8,128)(2,1)S(1)}, u32[]{:S(2)}, u32[]{:S(2)}) collective-permute-start(bf16[128,512]{1,0:T(8,128)(2,1)S(1)} %get-tuple-element.60), channel_id=1, source_target_pairs={{0,384},{128,0},{256,128},{384,256},{1,385},{129,1},{257,129},{385... | collective-permute-start | bytes 393224 | tf_op jit(solution)/shard_map/total/ppermute | solution.py:243
  35.3 3.4 %collective-permute-start.3 = (bf16[16,16,512]{2,1,0:T(8,128)(2,1)S(1)}, bf16[16,16,512]{2,1,0:T(8,128)(2,1)S(1)}, u32[]{:S(2)}, u32[]{:S(2)}) collective-permute-start(bf16[16,16,512]{2,1,0:T(8,128)(2,1)S(1)} %all-to-all-done.own_ref), channel_id=1, source_target_pairs={{0,4},{4,0},{1,5},{5,1},{2,6},{6,2},{3,7},{7,3},{8,12},{12,8},{9,1... | collective-permute-start | bytes 786440 | tf_op jit(solution)/shard_map/total/ppermute | solution.py:215
  55.9 12.1 %all-to-all-start.2 = ((f32[16,8,512]{2,1,0:T(8,128)}), f32[16,8,512]{2,1,0:T(8,128)S(1)}, u32[]{:S(2)}, u32[]{:S(2)}) async-start(f32[16,8,512]{2,1,0:T(8,128)} %broadcast_in_dim.19), calls=%async_computation.2 | async-start | bytes 524288 | tf_op jit(solution)/shard_map/left/all_to_all | solution.py:207
  69.6 3.8 %collective-permute-start.4 = (f32[1064,128]{1,0:T(8,128)S(1)}, f32[1064,128]{1,0:T(8,128)S(1)}, u32[]{:S(2)}, u32[]{:S(2)}) collective-permute-start(f32[1064,128]{1,0:T(8,128)S(1)} %get-tuple-element.38), channel_id=1, source_target_pairs={{0,4},{4,0},{1,5},{5,1},{2,6},{6,2},{3,7},{7,3},{8,12},{12,8},{9,1... | collective-permute-start | bytes 1634312 | tf_op jit(solution)/shard_map/products/ppermute | solution.py:215
  74.4 18.5 %all-to-all-start.3 = ((f32[4,296,128]{2,1,0:T(8,128)}), f32[4,296,128]{2,1,0:T(8,128)S(1)}, u32[]{:S(2)}, u32[]{:S(2)}) async-start(f32[4,296,128]{2,1,0:T(8,128)} %pad_maximum_fusion), calls=%async_computation.3 | async-start | bytes 1212416 | tf_op jit(solution)/shard_map/products/all_to_all | solution.py:207
  79.3 9.7 %collective-permute-start.6 = (f32[128,512]{1,0:T(8,128)S(1)}, f32[128,512]{1,0:T(8,128)S(1)}, u32[]{:S(2)}, u32[]{:S(2)}) collective-permute-start(f32[128,512]{1,0:T(8,128)S(1)} %get-tuple-element.36.total_ref.refs_0_), channel_id=1, source_target_pairs={{0,384},{128,0},{256,128},{384,256},{1,385},{129,1},{257,129},{385... | collective-permute-start | bytes 786440 | tf_op jit(solution)/shard_map/totals/ppermute | solution.py:258
  82.3 10.6 %collective-permute-start.5 = (f32[128,512]{1,0:T(8,128)S(1)}, f32[128,512]{1,0:T(8,128)S(1)}, u32[]{:S(2)}, u32[]{:S(2)}) collective-permute-start(f32[128,512]{1,0:T(8,128)S(1)} %get-tuple-element.36.total_ref.refs_0_), channel_id=1, source_target_pairs={{0,128},{128,256},{256,384},{384,0},{1,129},{129,257},{257,385},{3... | collective-permute-start | bytes 786440 | tf_op jit(solution)/shard_map/totals/ppermute | solution.py:258
  93.7 25.0 %all-to-all-start.4 = ((f32[4,104,128]{2,1,0:T(8,128)}), f32[4,104,128]{2,1,0:T(8,128)S(1)}, u32[]{:S(2)}, u32[]{:S(2)}) async-start(f32[4,104,128]{2,1,0:T(8,128)} %pad_maximum_fusion.1), calls=%async_computation.4 | async-start | bytes 425984 | tf_op jit(solution)/shard_map/products/all_to_all | solution.py:207
  101.8 10.3 %collective-permute-start.7 = (f32[128,512]{1,0:T(8,128)S(1)}, f32[128,512]{1,0:T(8,128)S(1)}, u32[]{:S(2)}, u32[]{:S(2)}) collective-permute-start(f32[128,512]{1,0:T(8,128)S(1)} %get-tuple-element.36.total_ref.refs_0_), channel_id=1, source_target_pairs={{0,256},{128,384},{256,0},{384,128},{1,257},{129,385},{257,1},{385... | collective-permute-start | bytes 786440 | tf_op jit(solution)/shard_map/totals/ppermute | solution.py:258
  119.5 12.5 %all-to-all-start.5 = ((f32[16,40,128]{2,1,0:T(8,128)}), f32[16,40,128]{2,1,0:T(8,128)S(1)}, u32[]{:S(2)}, u32[]{:S(2)}) async-start(f32[16,40,128]{2,1,0:T(8,128)} %broadcast_in_dim.22), calls=%async_computation.5 | async-start | bytes 655360 | tf_op jit(solution)/shard_map/products/all_to_all | solution.py:207
  132.0 7.7 %collective-permute-start.8 = (f32[16,40,128]{2,1,0:T(8,128)S(1)}, f32[16,40,128]{2,1,0:T(8,128)S(1)}, u32[]{:S(2)}, u32[]{:S(2)}) collective-permute-start(f32[16,40,128]{2,1,0:T(8,128)S(1)} %all-to-all-done.5.own_ref), channel_id=1, source_target_pairs={{0,4},{4,0},{1,5},{5,1},{2,6},{6,2},{3,7},{7,3},{8,12},{12,8},{9,1... | collective-permute-start | bytes 983048 | tf_op jit(solution)/shard_map/factor/ppermute | solution.py:215
  134.6 19.5 %all-to-all-start.6 = ((f32[4,64,128]{2,1,0:T(8,128)}), f32[4,64,128]{2,1,0:T(8,128)S(1)}, u32[]{:S(2)}, u32[]{:S(2)}) async-start(f32[4,64,128]{2,1,0:T(8,128)} %broadcast_in_dim.23), calls=%async_computation.6 | async-start | bytes 262144 | tf_op jit(solution)/shard_map/factor/all_to_all | solution.py:207
  149.3 0.9 copy-start.3
  155.0 20.1 %all-to-all-start.7 = ((f32[4,4,64,128]{3,2,1,0:T(8,128)}), f32[4,4,64,128]{3,2,1,0:T(8,128)S(1)}, u32[]{:S(2)}, u32[]{:S(2)}) async-start(f32[4,4,64,128]{3,2,1,0:T(8,128)} %broadcast_in_dim.24), calls=%async_computation.7 | async-start | bytes 1048576 | tf_op jit(solution)/shard_map/factor/all_to_all | solution.py:207
  161.7 1.1 copy-start.4
  174.2 0.8 copy-start.6
  175.1 3.8 %collective-permute-start.9 = (f32[16,4,16,128]{3,2,1,0:T(8,128)S(1)}, f32[16,4,16,128]{3,2,1,0:T(8,128)S(1)}, u32[]{:S(2)}, u32[]{:S(2)}) collective-permute-start(f32[16,4,16,128]{3,2,1,0:T(8,128)S(1)} %bitcast.24), channel_id=1, source_target_pairs={{0,4},{4,0},{1,5},{5,1},{2,6},{6,2},{3,7},{7,3},{8,12},{12,8},{9,1... | collective-permute-start | bytes 1572872 | tf_op jit(solution)/shard_map/right/ppermute | solution.py:215
  178.9 1.1 copy-start.5
  180.0 1.0 copy-start.7
  183.5 1.0 copy-start.1
  185.2 11.3 %all-to-all-start.8 = ((f32[16,1,512]{2,1,0:T(1,128)}), f32[16,1,512]{2,1,0:T(1,128)S(1)}, u32[]{:S(2)}, u32[]{:S(2)}) async-start(f32[16,1,512]{2,1,0:T(1,128)} %broadcast_in_dim.26), calls=%async_computation.8 | async-start | bytes 65536 | tf_op jit(solution)/shard_map/norms/all_to_all | solution.py:207
  196.5 1.2 copy-start.2
